TPU v7x, 256 devices: a whole 4x4x8 slice. The times are simulated.
256 devices in a mesh: blk: 64 (over z, x, core), reg: 4 (over y).
Axes of the slice: x: 4, y: 4, z: 8, core: 2. Of those that a mesh axis runs over, the one named last changes fastest.
Arguments:
- coefficients: bfloat16 [256, 2048, 256], P('blk'), may hold values from -0.1875 to 0.1875
- legendre: bfloat16 [256, 64, 4, 2, 2048], P('blk', None, 'reg'), may hold values from -0.125 to 0.125
- harmonic_orders: int32 [256], replicated, may hold values from 0 to 2047, as said below
- observed: float32 [512, 4096], P(('blk', 'reg')), may hold values from -6 to 6
- hole_rows: int32 [512, 4096], P(('blk', 'reg')), may hold values from -1 to 511, as said below
- boundary: int32 [64, 4, 256], P('blk'), may hold values from 0 to 32767, as said below
- tile_owner: int32 [64, 4], P('blk'), may hold values from 0 to 3, each once within a row
- kriging: bfloat16 [64, 4, 512, 256], P('blk', 'reg'), may hold values from -0.375 to 0.375
Outputs:
- filled: bfloat16 [128, 512, 4096], P(None, ('blk', 'reg'))
Inputs may be any that keep to these rules, and one draw needn't show every extreme that they name: `harmonic_orders`: distinct orders; both 0 and 2047 occur. `hole_rows`: the holes of region k of group b lie in cycles (b * 4 + k) * 2 to (b * 4 + k + 1) * 2 - 1; a region with n hole pixels numbers them 0 to n - 1, once each; in every group one region has exactly 512 hole pixels. `boundary`: the 256 pixels of a region are distinct, lie in its group's cycles, and none is a hole pixel; entries i with i // 64 = d lie in cycles (b * 4 + d) * 2 to (b * 4 + d + 1) * 2 - 1. `tile_owner`: each row is a permutation of 0 to 3.
All inputs are finite; a program needn't handle non-finite values.
Results may differ from a plain program's by a relative error of at most 0.0032.
Values may be sent and summed in bfloat16 or wider, within the bound.
No kernel may reach another device: no remote copies, remote signals or barrier semaphores. Data moves between devices by JAX's collectives and lax.ppermute only.
A program may use at most 64 MiB of HBM per device.

v0:
```python
import math

import jax
import jax.numpy as jnp
from jax import lax
from jax.sharding import PartitionSpec as P


def phase_table(harmonic_orders, cycle_pixels):
    columns = jnp.arange(cycle_pixels, dtype=jnp.int32)
    phase_steps = harmonic_orders[:, None] * columns[None, :] % cycle_pixels
    angles = phase_steps.astype(jnp.float32) * (2.0 * math.pi / cycle_pixels)
    weights = jnp.where(harmonic_orders == 0, 1.0, 2.0).astype(jnp.float32)[:, None]
    return jnp.stack([weights * jnp.cos(angles), -weights * jnp.sin(angles)]).astype(jnp.bfloat16)


def cycle_synthesis(spectra, phases):
    orders = spectra.shape[0]
    cycle_count = spectra.shape[3]
    halves = spectra.reshape(orders, cycle_count, 2, spectra.shape[4] // 2)
    return jnp.einsum("mrcs,cmp->srp", halves, phases, preferred_element_type=jnp.float32).astype(
        jnp.bfloat16
    )


def body(
    coefficients, legendre, harmonic_orders, observed, hole_rows, boundary, tile_owner, kriging
):
    reg_index = lax.axis_index("reg")
    local_orders = legendre.shape[0]
    block_count = legendre.shape[1]
    cycle_count = legendre.shape[3]
    degrees = legendre.shape[4]
    samples = coefficients.shape[2] // 2
    cycle_pixels = observed.shape[1]
    device_pixels = cycle_count * cycle_pixels
    regions = boundary.shape[1]
    edge_count = boundary.shape[2]
    slot_count = edge_count // regions
    phases = phase_table(harmonic_orders, cycle_pixels)
    folded = legendre.reshape(local_orders, block_count * cycle_count, degrees)
    spectra = lax.dot_general(
        folded, coefficients, (((2,), (1,)), ((0,), (0,))), preferred_element_type=jnp.float32
    )
    spectra = spectra.astype(jnp.bfloat16).reshape(
        local_orders, block_count, 1, cycle_count, 2 * samples
    )
    edge_mine = lax.dynamic_slice_in_dim(boundary[0], reg_index * slot_count, slot_count, 1)
    edge_local = edge_mine.reshape(regions * slot_count) - reg_index * device_pixels
    edge_clip = jnp.clip(edge_local, 0, device_pixels - 1)
    observed_flat = observed.reshape(device_pixels)
    sky_map = (lambda spectra_part: cycle_synthesis(spectra_part, phases))(
        lax.all_to_all(spectra, "blk", split_axis=1, concat_axis=0, tiled=True)
    )
    edge_sky = jnp.take(sky_map.reshape(samples, device_pixels), edge_clip, axis=1)
    residual = observed_flat[edge_clip][None, :] - edge_sky.astype(jnp.float32)
    residual = (
        residual.astype(jnp.bfloat16).reshape(samples, regions, slot_count).transpose(1, 0, 2)
    )
    owners = tile_owner[0]
    my_owner = lax.dynamic_index_in_dim(owners, reg_index, 0, keepdims=False)
    mine_mask = owners == reg_index
    home_edges = lax.all_to_all(residual, "reg", split_axis=0, concat_axis=2, tiled=True)
    tile_here = kriging[0, 0]
    outgoing = jnp.where(mine_mask[:, None, None], tile_here[None], jnp.zeros_like(tile_here)[None])
    every_tile = lax.all_to_all(outgoing, "reg", split_axis=0, concat_axis=0, tiled=True)
    my_tile = lax.dynamic_index_in_dim(every_tile, my_owner, 0, keepdims=False)
    correction = jnp.einsum(
        "hi,si->sh", my_tile, home_edges[0], preferred_element_type=jnp.float32
    ).astype(jnp.bfloat16)
    holes_flat = hole_rows.reshape(device_pixels)
    picked = jnp.take(correction, jnp.maximum(holes_flat, 0), axis=1).reshape(
        samples, cycle_count, cycle_pixels
    )
    filled = jnp.where(
        (hole_rows >= 0)[None],
        sky_map.astype(jnp.float32) + picked.astype(jnp.float32),
        observed[None],
    )
    return filled.astype(jnp.bfloat16)


def solution(mesh):
    return jax.shard_map(
        body,
        mesh=mesh,
        in_specs=(
            P("blk", None, None),
            P("blk", None, "reg", None, None),
            P(),
            P(("blk", "reg"), None),
            P(("blk", "reg"), None),
            P("blk", None, None),
            P("blk", None),
            P("blk", "reg", None, None),
        ),
        out_specs=P(None, ("blk", "reg"), None),
        check_vma=False,
    )
```

profile of v0, /device:TPU:1, one launch (start us, length us, event | category | flops | bytes accessed | tf_op | source)
XLA Modules:
  0.0 108.9 jit_solution(11966368367623437554)
XLA Ops:
  0.0 2.7 %reshape.244 = bf16[4,128,2048]{2,1,0:T(8,128)(2,1)S(1)} reshape(bf16[4,64,1,2,2048]{4,3,2,1,0:T(2,128)(2,1)} %param.9) | data formatting | bytes 4194304 | tf_op jit(solution)/shard_map/reshape | solution.py:41
  2.8 0.0 copy-start.4
  2.8 0.0 copy-start.5
  2.8 0.0 copy-start.3
  2.8 2.9 %convolution_convert_fusion = bf16[4,128,256]{2,1,0:T(8,128)(2,1)S(1)} fusion(bf16[4,128,2048]{2,1,0:T(8,128)(2,1)S(1)} %reshape.244, bf16[4,2048,256]{2,1,0:T(8,128)(2,1)} %param.8), kind=kOutput, calls=%fused_computation.20 | convolution fusion | flops 537001984 | bytes 6553600 | tf_op jit(solution)/shard_map/dot_general | solution.py:42
  5.7 0.0 copy-start.2
  5.7 0.0 copy-start.6
  5.7 0.0 copy-start.1
  5.7 0.1 reshape.245
  5.9 0.9 copy.15
  6.7 13.0 %all-to-all-start = ((bf16[4,64,1,2,256]{4,3,0,2,1:T(2,128)(2,1)}), bf16[4,64,1,2,256]{4,3,0,2,1:T(2,128)(2,1)S(1)}, u32[]{:S(2)}, u32[]{:S(2)}) async-start(bf16[4,64,1,2,256]{4,3,0,2,1:T(2,128)(2,1)} %copy.15), calls=%async_computation | async-start | bytes 524288 | tf_op jit(solution)/shard_map/all_to_all | solution.py:53
  19.7 0.0 copy-done.4
  19.8 0.0 copy-done.5
  19.8 0.1 compare_and_fusion
  19.9 0.1 min.16
  20.0 0.0 copy-done.3
  20.0 18.4 %multiply_convert_fusion.1 = (bf16[1,256,4096]{1,2,0:T(8,128)(2,1)}, bf16[1,256,4096]{1,2,0:T(8,128)(2,1)}) fusion(s32[256]{0:T(256)S(1)} %copy-done.4, f32[256]{0:T(256)S(1)} %get-tuple-element.11, f32[256]{0:T(256)S(1)} %get-tuple-element.12), kind=kLoop, calls=%fused_computation.16 | loop fusion | flops 18874368 | bytes 4197376 | tf_op jit(solution)/shard_map/convert
  38.4 0.0 copy-done.2
  38.4 1.7 %gather_fusion = f32[256]{0:T(256)S(1)} fusion(f32[8192]{0:T(1024)S(1)} %bitcast.50, s32[1024]{0:T(1024)S(1)} %pad_clamp_fusion), kind=kCustom, calls=%fused_computation | custom fusion | bytes 3072 | tf_op jit(solution)/shard_map/gather | solution.py:56
  40.1 0.1 sub.31
  40.2 0.0 copy-done.6
  40.2 0.0 copy-done.1
  40.2 1.1 %broadcast_select_fusion = bf16[4,512,256]{2,1,0:T(8,128)(2,1)} fusion(pred[4]{0:T(512)(128)(4,1)S(1)} %compare_bitcast_fusion, bf16[512,256]{1,0:T(8,128)(2,1)S(1)} %bitcast.54), kind=kLoop, calls=%fused_computation.22 | loop fusion | flops 524288 | bytes 1310724 | tf_op jit(solution)/shard_map/jit(_where)/select_n | solution.py:65
  41.3 0.0 all-to-all-done
  41.3 0.2 reshape.246
  41.5 3.5 %fusion = bf16[4096,2,128]{2,0,1:T(8,128)(2,1)S(1)} fusion(bf16[1,256,4096]{1,2,0:T(8,128)(2,1)} %get-tuple-element.10, bf16[1,256,4096]{1,2,0:T(8,128)(2,1)} %get-tuple-element.9, bf16[256,2,2,128]{3,2,1,0:T(2,128)(2,1)S(1)} %reshape.246), kind=kOutput, calls=%fused_computation.7 | convolution fusion | flops 1083179008 | bytes 6553600 | tf_op jit(solution)/shard_map/mrcs,cmp->srp/dot_general | solution.py:21
  45.0 0.0 copy-start
  45.0 0.9 gather_fusion.1
  45.9 0.8 fusion.12
  46.6 4.2 %all-to-all-start.1 = ((bf16[4,128,64]{1,2,0:T(8,128)(2,1)}), bf16[4,128,64]{1,2,0:T(8,128)(2,1)S(1)}, u32[]{:S(2)}, u32[]{:S(2)}) async-start(bf16[4,128,64]{1,2,0:T(8,128)(2,1)} %fusion.12), calls=%async_computation.1 | async-start | bytes 131072 | tf_op jit(solution)/shard_map/all_to_all | solution.py:63
  50.8 0.6 constant_dynamic-slice_fusion
  53.1 2.2 %all-to-all-done.1 = bf16[4,128,64]{1,2,0:T(8,128)(2,1)S(1)} async-done(((bf16[4,128,64]{1,2,0:T(8,128)(2,1)}), bf16[4,128,64]{1,2,0:T(8,128)(2,1)S(1)}, u32[]{:S(2)}, u32[]{:S(2)}) %all-to-all-start.1) | async-done | bytes 65568 | tf_op jit(solution)/shard_map/all_to_all | solution.py:63
  55.3 3.5 %all-to-all-start.2 = ((bf16[4,512,256]{2,1,0:T(8,128)(2,1)}), bf16[4,512,256]{2,1,0:T(8,128)(2,1)S(1)}, u32[]{:S(2)}, u32[]{:S(2)}) async-start(bf16[4,512,256]{2,1,0:T(8,128)(2,1)} %broadcast_select_fusion), calls=%async_computation.2 | async-start | bytes 2097152 | tf_op jit(solution)/shard_map/all_to_all | solution.py:66
  58.8 13.2 %all-to-all-done.2 = bf16[4,512,256]{2,1,0:T(8,128)(2,1)S(1)} async-done(((bf16[4,512,256]{2,1,0:T(8,128)(2,1)}), bf16[4,512,256]{2,1,0:T(8,128)(2,1)S(1)}, u32[]{:S(2)}, u32[]{:S(2)}) %all-to-all-start.2) | async-done | bytes 1048608 | tf_op jit(solution)/shard_map/all_to_all | solution.py:66
  72.0 0.2 convolution_convert_fusion.1
  72.2 0.0 copy-done
  72.2 0.1 copy.17
  72.4 24.0 %gather_fusion.2 = bf16[8192,128]{1,0:T(8,128)(2,1)S(1)} fusion(bf16[128,512]{0,1:T(8,128)(2,1)S(1)} %copy.17, s32[8192]{0:T(1024)S(1)} %broadcast_clamp_fusion), kind=kCustom, calls=%fused_computation.2 | custom fusion | bytes 4227072 | tf_op jit(solution)/shard_map/jit(_take)/gather | solution.py:72
  96.4 6.4 %select_convert_fusion = bf16[128,2,4096]{0,2,1:T(8,128)(2,1)} fusion(bf16[4096,2,128]{2,0,1:T(8,128)(2,1)} %copy-done, f32[2,4096]{1,0:T(2,128)S(1)} %copy-done.2, bf16[128,2,4096]{0,2,1:T(8,128)(2,1)S(1)} %bitcast.51, pred[2,4096]{1,0:T(4,128)(4,1)S(1)} %get-tuple-element.8, pred[2,4096]{1,0:T(4,128)(4,1)S(1)} %get-tuple-element.7), kind=kLoop, calls=%fused_computation.14 | loop fusion | flops 5242880 | bytes 6340608 | tf_op jit(solution)/shard_map/convert_element_type | solution.py:80
  102.8 6.2 %copy.18 = bf16[128,2,4096]{2,1,0:T(2,128)(2,1)} copy(bf16[128,2,4096]{0,2,1:T(8,128)(2,1)} %select_convert_fusion) | data formatting | bytes 4194304 | tf_op jit(solution)/shard_map/convert_element_type | solution.py:80
  (9 shorter events, 0.1 us)
Async XLA Ops:
  2.8 17.0 %copy-start.4 = (s32[256]{0:T(256)S(1)}, s32[256]{0:T(256)}, u32[]{:S(2)}) copy-start(s32[256]{0:T(256)} %param.10) | copy-start | bytes 3076
  2.8 17.0 %copy-start.5 = (s32[1,4,256]{2,1,0:T(4,128)S(1)}, s32[1,4,256]{2,1,0:T(4,128)}, u32[]{:S(2)}) copy-start(s32[1,4,256]{2,1,0:T(4,128)} %param.13) | copy-start | bytes 12292
  2.8 17.2 %copy-start.3 = (s32[2,4096]{1,0:T(2,128)S(1)}, s32[2,4096]{1,0:T(2,128)}, u32[]{:S(2)}) copy-start(s32[2,4096]{1,0:T(2,128)} %param.12) | copy-start | bytes 98308
  5.7 32.7 %copy-start.2 = (f32[2,4096]{1,0:T(2,128)S(1)}, f32[2,4096]{1,0:T(2,128)}, u32[]{:S(2)}) copy-start(f32[2,4096]{1,0:T(2,128)} %param.11) | copy-start | bytes 98308
  5.7 34.5 %copy-start.6 = (s32[1,4]{1,0:T(1,128)S(1)}, s32[1,4]{1,0:T(1,128)}, u32[]{:S(2)}) copy-start(s32[1,4]{1,0:T(1,128)} %param.14) | copy-start | bytes 52
  5.7 34.5 %copy-start.1 = (bf16[1,1,512,256]{3,2,1,0:T(8,128)(2,1)S(1)}, bf16[1,1,512,256]{3,2,1,0:T(8,128)(2,1)}, u32[]{:S(2)}) copy-start(bf16[1,1,512,256]{3,2,1,0:T(8,128)(2,1)} %param.15) | copy-start | bytes 786436
  6.7 34.6 %all-to-all-start = ((bf16[4,64,1,2,256]{4,3,0,2,1:T(2,128)(2,1)}), bf16[4,64,1,2,256]{4,3,0,2,1:T(2,128)(2,1)S(1)}, u32[]{:S(2)}, u32[]{:S(2)}) async-start(bf16[4,64,1,2,256]{4,3,0,2,1:T(2,128)(2,1)} %copy.15), calls=%async_computation | async-start | bytes 524288 | tf_op jit(solution)/shard_map/all_to_all | solution.py:53
  45.0 27.2 %copy-start = (bf16[4096,2,128]{2,0,1:T(8,128)(2,1)}, bf16[4096,2,128]{2,0,1:T(8,128)(2,1)S(1)}, u32[]{:S(2)}) copy-start(bf16[4096,2,128]{2,0,1:T(8,128)(2,1)S(1)} %fusion) | copy-start | bytes 6291460
  46.6 8.6 %all-to-all-start.1 = ((bf16[4,128,64]{1,2,0:T(8,128)(2,1)}), bf16[4,128,64]{1,2,0:T(8,128)(2,1)S(1)}, u32[]{:S(2)}, u32[]{:S(2)}) async-start(bf16[4,128,64]{1,2,0:T(8,128)(2,1)} %fusion.12), calls=%async_computation.1 | async-start | bytes 131072 | tf_op jit(solution)/shard_map/all_to_all | solution.py:63
  55.3 16.7 %all-to-all-start.2 = ((bf16[4,512,256]{2,1,0:T(8,128)(2,1)}), bf16[4,512,256]{2,1,0:T(8,128)(2,1)S(1)}, u32[]{:S(2)}, u32[]{:S(2)}) async-start(bf16[4,512,256]{2,1,0:T(8,128)(2,1)} %broadcast_select_fusion), calls=%async_computation.2 | async-start | bytes 2097152 | tf_op jit(solution)/shard_map/all_to_all | solution.py:66
where the time goes:
time: 111 us; the launch traced here: 109 us
  local copies, waits for them, and re-layouts  37.6 us (34%)
  other arithmetic  26.8 us (24%)
  starting transfers between devices  20.7 us (19%)
  waiting for transfers between devices  15.3 us (14%)
  matrix products  6.62 us (6%)
  between operations  1.91 us (2%)
    gather x1, local copies, waits for them, and re-layouts, body(): jnp.take(correction, jnp.maximum(holes_flat, 0), axis=1)  24 us
    another operation x1, other arithmetic  18.4 us
    all_to_all x1, waiting for transfers between devices, body(): lax.all_to_all(outgoing, 'reg', split_axis=0, concat_axis=0, tiled=True)  13.2 us
    all_to_all x1, starting transfers between devices, body(): lax.all_to_all(spectra, 'blk', split_axis=1, concat_axis=0, tiled=True)  13 us
    convert_element_type x1, other arithmetic, body(): return filled.astype(jnp.bfloat16)  6.37 us
    convert_element_type x1, local copies, waits for them, and re-layouts, body(): return filled.astype(jnp.bfloat16)  6.16 us
    all_to_all x1, starting transfers between devices, body(): lax.all_to_all(residual, 'reg', split_axis=0, concat_axis=2, tiled=True)  4.17 us
    all_to_all x1, starting transfers between devices, body(): lax.all_to_all(outgoing, 'reg', split_axis=0, concat_axis=0, tiled=True)  3.52 us
  transfers between devices with their start and end apart: 3, of which 2 were waited for; matrix products, arithmetic and copies ran while one was open for 20% of the time, Pallas kernels for 0%

commit v1 on v0

v1 whole, which is shorter than its diff:
```python
import functools

import jax
import jax.numpy as jnp
from jax import lax
from jax.experimental import pallas as pl
from jax.experimental.pallas import tpu as pltpu
from jax.sharding import PartitionSpec as P

BF = jnp.bfloat16
F32 = jnp.float32
I32 = jnp.int32
NBLK = 64
NREG = 4
NM = 4
L = 2048
KT = L // 128
NPHI = 4096
NG = 2 * NPHI // 128
NB = 256
SLOTS = NB // NREG
HMAX = 512
NS = 128
NK = NBLK * 16
MB = 1024 * 1024
ROUND = 12582912.0
COS = (
    0.9999999890590234,
    -19.739204499453898,
    64.93911745989367,
    -85.45013953084099,
    60.16763095056212,
    -25.967599246900118,
    6.528658158989,
)


def vmem():
    return pl.BlockSpec(memory_space=pltpu.VMEM)


def smem():
    return pl.BlockSpec(memory_space=pltpu.SMEM)


def anywhere():
    return pl.BlockSpec(memory_space=pl.ANY)


def params(mib):
    return pltpu.CompilerParams(vmem_limit_bytes=mib * MB)


def iota(shape, axis):
    return lax.broadcasted_iota(I32, shape, axis)


def dot(a, b):
    return jnp.dot(a, b, preferred_element_type=F32)


def dot_nt(a, b):
    return lax.dot_general(a, b, (((1,), (1,)), ((), ())), preferred_element_type=F32)


def legendre_kernel(leg, coef, out, legv, coefv, resv, lsem, csem, osem):
    def coef_copy(m):
        return pltpu.make_async_copy(coef.at[m], coefv.at[m], csem.at[m])

    for m in range(NM):
        for k in range(KT):
            pltpu.make_async_copy(leg.at[m, :, k], legv.at[m, k], lsem.at[m]).start()
        coef_copy(m).start()
    for m in range(NM):
        pltpu.make_async_copy(legv.at[m], legv.at[m], lsem.at[m]).wait()
        coef_copy(m).wait()
        total = jnp.zeros((2 * NBLK, 2 * NS), F32)
        for k in range(KT // 2):
            pair = [legv.at[m, 2 * k + i].reshape(2 * NBLK, 128)[...] for i in range(2)]
            total += dot(jnp.concatenate(pair, axis=1), coefv[m, k * 256 : (k + 1) * 256, :])
        rounded = total.astype(BF)
        for c in range(2):
            resv.at[m, c].reshape(2 * NBLK, 128)[...] = rounded[:, c * 128 : (c + 1) * 128]
            pltpu.make_async_copy(resv.at[m, c], out.at[:, c, m], osem).start()
    pltpu.make_async_copy(resv, resv, osem).wait()


def legendre_sums(legendre, coefficients):
    view = legendre.reshape(NM, NBLK, 2, KT, 128).transpose(0, 1, 3, 2, 4)
    return pl.pallas_call(
        legendre_kernel,
        out_shape=jax.ShapeDtypeStruct((NBLK, 2, NM, 2, 128), BF),
        in_specs=[anywhere(), anywhere()],
        out_specs=anywhere(),
        scratch_shapes=[
            pltpu.VMEM((NM, KT, NBLK, 2, 128), BF),
            pltpu.VMEM((NM, L, 2 * NS), BF),
            pltpu.VMEM((NM, 2, NBLK, 2, 128), BF),
            pltpu.SemaphoreType.DMA((NM,)),
            pltpu.SemaphoreType.DMA((NM,)),
            pltpu.SemaphoreType.DMA,
        ],
        compiler_params=params(60),
        cost_estimate=pl.CostEstimate(flops=2 * NM * 128 * L * 256, bytes_accessed=6 * MB, transcendentals=0),
        name="legendre_sums",
    )(view, coefficients)


def prepare_kernel(reg, holes, observed, boundary, orders, pb, ph, obsb, grp, lan, obsm, amat, bmat, pcol, rcol, rows):
    me = reg[0]
    h = holes[...].reshape(NG, 128)
    obs = observed[...].reshape(NG, 128)
    obsm[...] = jnp.where(h >= 0, 0.0, obs).astype(BF)

    hi, lo = h >> 4, h & 15
    a_iota, b_iota, lane = iota((32, 128), 0), iota((16, 128), 0), iota((32, 128), 1).astype(F32)
    for g in range(NG):
        hit = a_iota == hi[g : g + 1, :]
        at = pl.ds(g * 128, 128)
        amat[0:32, at] = jnp.where(hit, float(g + 1), 0.0).astype(BF)
        amat[32:64, at] = jnp.where(hit, lane, 0.0).astype(BF)
        bmat[:, at] = jnp.where(b_iota == lo[g : g + 1, :], 1.0, 0.0).astype(BF)
    tall = dot_nt(amat[...], bmat[...]).astype(BF)
    wide = dot_nt(bmat[...], amat[...]).astype(BF)
    pick = (iota((HMAX, 32), 0) // 16 == iota((HMAX, 32), 1)).astype(F32).astype(BF)
    low = iota((HMAX, 16), 0) % 16 == iota((HMAX, 16), 1)
    g1 = jnp.sum(jnp.where(low, dot(pick, tall[0:32]), 0.0), axis=1, keepdims=True)
    lh = jnp.sum(jnp.where(low, dot(pick, tall[32:64]), 0.0), axis=1, keepdims=True)
    pick_t = (iota((32, HMAX), 1) // 16 == iota((32, HMAX), 0)).astype(F32).astype(BF)
    low_t = iota((16, HMAX), 1) % 16 == iota((16, HMAX), 0)
    g1_row = jnp.sum(jnp.where(low_t, dot(wide[:, 0:32], pick_t), 0.0), axis=0, keepdims=True)
    grp[...] = jnp.where((iota((NG, HMAX), 0) + 1).astype(F32) == g1_row, 1.0, 0.0).astype(BF)
    lan[...] = jnp.where(iota((HMAX, 128), 1).astype(F32) == lh, 1.0, 0.0).astype(BF)
    gh = g1 - 1.0
    tile_h = jnp.floor(gh * 0.5)
    pcol[NB:, :] = jnp.broadcast_to(tile_h * 128.0 + lh, (HMAX, 128))
    rcol[NB:, :] = jnp.broadcast_to(gh - 2.0 * tile_h, (HMAX, 128))

    mine = iota((SLOTS, NB), 1) == iota((SLOTS, NB), 0) + me * SLOTS
    cols = []
    for d in range(NREG):
        line = boundary[pl.ds(lax.rem(me + d, NREG), 1), :].astype(F32)
        cols.append(jnp.sum(jnp.where(mine, line, 0.0), axis=1, keepdims=True))
    u = jnp.concatenate(cols, axis=0) - (me * (2 * NPHI)).astype(F32)
    rb = jnp.where(u >= float(NPHI), 1.0, 0.0)
    p = u - rb * float(NPHI)
    tile_b = jnp.floor(p * (1.0 / 128.0))
    lane_b = p - tile_b * 128.0
    pcol[0:NB, :] = jnp.broadcast_to(p, (NB, 128))
    rcol[0:NB, :] = jnp.broadcast_to(rb, (NB, 128))
    one = jnp.where(iota((NB, NG), 1).astype(F32) == 2.0 * tile_b + rb, 1.0, 0.0).astype(BF)
    first = obs.astype(BF)
    rest = obs - first.astype(F32)
    second = rest.astype(BF)
    third = (rest - second.astype(F32)).astype(BF)
    value = dot(one, first) + dot(one, second) + dot(one, third)
    value = jnp.where(iota((NB, 128), 1).astype(F32) == lane_b, value, 0.0)
    obsb[...] = jnp.broadcast_to(jnp.sum(value, axis=1, keepdims=True), (NB, 128))

    line = jnp.broadcast_to(orders[...], (8, 256))
    split = jnp.concatenate([(line >> 3).astype(F32), (line & 7).astype(F32)], axis=0).astype(BF)
    at = iota((256, NK), 1)
    spread = (iota((256, NK), 0) == (at >> 4) * 4 + ((at & 7) >> 1)).astype(F32).astype(BF)
    both = dot(split, spread)
    order = both[0:8] * 8.0 + both[8:16]
    at = iota((8, NK), 1)
    rows[0] = order * (1.0 / NPHI)
    rows[1] = ((at >> 3) & 1).astype(F32) * 0.25
    rows[2] = (at & 1).astype(F32)
    rows[3] = jnp.where(order == 0.0, 1.0, 2.0)

    def phases(out, base):
        def step(i, _):
            at = pl.multiple_of(i * 16, 16)
            pc = pcol[pl.ds(base + at, 16), :]
            rc = rcol[pl.ds(base + at, 16), :]
            for t in range(NK // 128):
                ls = slice(t * 128, (t + 1) * 128)
                turn = pc * rows[0, 0:1, ls] + rows[1, 0:1, ls]
                turn = turn - ((turn + ROUND) - ROUND)
                z = turn * turn
                value = jnp.full((16, 128), COS[-1], F32)
                for c in COS[-2::-1]:
                    value = value * z + c
                weight = jnp.where(rc == rows[2, 0:1, ls], rows[3, 0:1, ls], 0.0)
                out[pl.ds(at, 16), ls] = (value * weight).astype(BF)
            return 0

        lax.fori_loop(0, out.shape[0] // 16, step, 0)

    phases(pb, 0)
    phases(ph, NB)


def prepare(reg, holes, observed, boundary, orders):
    shapes = [
        ((NB, NK), BF),
        ((HMAX, NK), BF),
        ((NB, 128), F32),
        ((NG, HMAX), BF),
        ((HMAX, 128), BF),
        ((NG, 128), BF),
    ]
    return pl.pallas_call(
        prepare_kernel,
        out_shape=[jax.ShapeDtypeStruct(s, t) for s, t in shapes],
        in_specs=[smem()] + [vmem()] * 4,
        out_specs=[vmem()] * 6,
        scratch_shapes=[
            pltpu.VMEM((64, 2 * NPHI), BF),
            pltpu.VMEM((16, 2 * NPHI), BF),
            pltpu.VMEM((NB + HMAX, 128), F32),
            pltpu.VMEM((NB + HMAX, 128), F32),
            pltpu.VMEM((4, 8, NK), F32),
        ],
        compiler_params=params(30),
        cost_estimate=pl.CostEstimate(flops=20_000_000, bytes_accessed=8 * MB, transcendentals=0),
        name="prepare",
    )(reg, holes, observed, boundary, orders)


def residual_kernel(spectra, pb, obsb, own, to1, to2, to3):
    sky = dot(pb[...], spectra[...]).astype(BF).astype(F32)
    residual = (obsb[...] - sky).astype(BF)
    for d, ref in enumerate((own, to1, to2, to3)):
        ref[...] = residual[d * SLOTS : (d + 1) * SLOTS, :]


def residuals(spectra, pb, obsb):
    return pl.pallas_call(
        residual_kernel,
        out_shape=[jax.ShapeDtypeStruct((SLOTS, NS), BF)] * NREG,
        in_specs=[vmem()] * 3,
        out_specs=[vmem()] * NREG,
        compiler_params=params(30),
        cost_estimate=pl.CostEstimate(flops=2 * NB * NK * NS, bytes_accessed=MB, transcendentals=0),
        name="residuals",
    )(spectra, pb, obsb)


def hole_kernel(reg, owners, spectra, ph, tile0, tile1, tile2, tile3, after, sky, tile):
    del after
    sky[...] = dot(ph[...], spectra[...]).astype(BF)
    me = reg[0]
    away = lax.rem(me - owners[0, me] + NREG, NREG)
    for d, ref in enumerate((tile0, tile1, tile2, tile3)):

        @pl.when(away == d)
        def _(ref=ref):
            tile[...] = ref[...]


def hole_sky(reg, owners, spectra, ph, tiles, after):
    return pl.pallas_call(
        hole_kernel,
        out_shape=[jax.ShapeDtypeStruct((HMAX, NS), BF), jax.ShapeDtypeStruct((HMAX, NB), BF)],
        in_specs=[smem(), smem()] + [vmem()] * 6 + [anywhere()],
        out_specs=[vmem()] * 2,
        compiler_params=params(30),
        cost_estimate=pl.CostEstimate(flops=2 * HMAX * NK * NS, bytes_accessed=2 * MB, transcendentals=0),
        name="hole_sky",
    )(reg, owners, spectra, ph, *tiles, after)


CHUNK = 8


def fill_kernel(reg, own, from1, from2, from3, tile, sky, grp, lan, obsm, out, edge, xt, outv, sem):
    me = reg[0]
    for d, ref in enumerate((own, from1, from2, from3)):
        source = lax.rem(me - d + NREG, NREG)
        edge[pl.ds(pl.multiple_of(source * SLOTS, SLOTS), SLOTS), :] = ref[...]
    correction = dot(tile[...], edge[...]).astype(BF)
    holes = (sky[...].astype(F32) + correction.astype(F32)).astype(BF).astype(F32)
    xt[...] = holes.T
    groups = grp[...]
    lanes = lan[...]
    base = obsm[...]

    def copy(i):
        at = pl.ds(pl.multiple_of(i * (CHUNK * NG), CHUNK * NG), CHUNK * NG)
        return pltpu.make_async_copy(outv.at[at], out.at[at], sem)

    def step(i, _):
        parts = []
        for j in range(CHUNK):
            line = xt[pl.ds(i * CHUNK + j, 1), :].astype(BF)
            parts.append(groups * line)
        got = dot(jnp.concatenate(parts, axis=0), lanes).astype(BF)
        for j in range(CHUNK):
            at = pl.multiple_of(i * (CHUNK * NG) + j * NG, NG)
            outv[pl.ds(at, NG), :] = got[j * NG : (j + 1) * NG] + base
        copy(i).start()
        return 0

    lax.fori_loop(0, NS // CHUNK, step, 0)
    pltpu.make_async_copy(outv, outv, sem).wait()


def fill(reg, edges, tile, sky, grp, lan, obsm):
    return pl.pallas_call(
        fill_kernel,
        out_shape=jax.ShapeDtypeStruct((NS * NG, 128), BF),
        in_specs=[smem()] + [vmem()] * 9,
        out_specs=anywhere(),
        scratch_shapes=[
            pltpu.VMEM((NB, NS), BF),
            pltpu.VMEM((NS, HMAX), F32),
            pltpu.VMEM((NS * NG, 128), BF),
            pltpu.SemaphoreType.DMA,
        ],
        compiler_params=params(60),
        cost_estimate=pl.CostEstimate(flops=2 * NS * NG * HMAX * 128, bytes_accessed=3 * MB, transcendentals=0),
        name="fill",
    )(reg, *edges, tile, sky, grp, lan, obsm)


def by_lane_tile(x):
    return x.reshape(2, NPHI // 128, 128).transpose(1, 0, 2)


def shifted(x, d):
    return lax.ppermute(x, "reg", [(i, (i + d) % NREG) for i in range(NREG)])


def body(coefficients, legendre, harmonic_orders, observed, hole_rows, boundary, tile_owner, kriging):
    reg = lax.axis_index("reg").astype(I32).reshape(1)
    sums = legendre_sums(legendre, coefficients)
    spectra = lax.all_to_all(sums, "blk", split_axis=0, concat_axis=0, tiled=True).reshape(NK, 128)
    pb, ph, obsb, grp, lan, obsm = prepare(
        reg, by_lane_tile(hole_rows), by_lane_tile(observed), boundary.reshape(NREG, NB), harmonic_orders.reshape(1, -1)
    )
    tile = kriging.reshape(HMAX, NB)
    tiles = [tile] + [shifted(tile, d) for d in (1, 2, 3)]
    own, *away = residuals(spectra, pb, obsb)
    edges = [own] + [shifted(x, d + 1) for d, x in enumerate(away)]
    sky, my_tile = hole_sky(reg, tile_owner, spectra, ph, tiles, own)
    out = fill(reg, edges, my_tile, sky, grp, lan, obsm)
    return out.reshape(NS, NPHI // 128, 2, 128).transpose(0, 2, 1, 3).reshape(NS, 2, NPHI)


def solution(mesh):
    return jax.shard_map(
        body,
        mesh=mesh,
        in_specs=(
            P("blk", None, None),
            P("blk", None, "reg", None, None),
            P(),
            P(("blk", "reg"), None),
            P(("blk", "reg"), None),
            P("blk", None, None),
            P("blk", None),
            P("blk", "reg", None, None),
        ),
        out_specs=P(None, ("blk", "reg"), None),
        check_vma=False,
    )
```

time: 111 us -> 46.5 us (0.42); the launches traced: 109 us -> 46.4 us
  local copies, waits for them, and re-layouts: 37.6 us -> 3.82 us
  other arithmetic: 26.8 us -> 0 us
  Pallas kernels: 0 us -> 16.9 us
  waiting for transfers between devices: 15.3 us -> 2.33 us
  matrix products: 6.62 us -> 0 us
  starting transfers between devices: 20.7 us -> 23.1 us
  between operations: 1.91 us -> 0.15 us
    gather x3 -> x0, local copies, waits for them, and re-layouts: 26.6 us -> none  [the longest x1 24 us: body(): jnp.take(correction, jnp.maximum(holes_flat, 0), axis=1)]
    another operation x1 -> x0, other arithmetic: 18.4 us -> none
    pallas_call x0 -> x5, Pallas kernels: none -> 16.9 us  [the longest x1 7.09 us: fill(): pl.pallas_call(fill_kernel, out_shape=jax.ShapeDtypeStruct((NS * NG, 128)...]
    all_to_all x3 -> x1, waiting for transfers between devices: 15.3 us -> 2.31 us  [body(): lax.all_to_all(sums, 'blk', split_axis=0, concat_axis=0, tiled=True)]
    ppermute x0 -> x6, starting transfers between devices: none -> 10.1 us  [shifted(): return lax.ppermute(x, 'reg', [(i, (i + d) % NREG) for i in range(NREG)])]
    all_to_all x3 -> x1, starting transfers between devices: 20.7 us -> 13 us  [body(): lax.all_to_all(sums, 'blk', split_axis=0, concat_axis=0, tiled=True)]
    dot_general x3 -> x0, matrix products: 6.62 us -> none  [the longest x1 3.48 us: cycle_synthesis(): jnp.einsum('mrcs,cmp->srp', halves, phases, preferred_element_type=jnp.fl...]
    convert_element_type x1 -> x0, other arithmetic: 6.37 us -> none  [body(): return filled.astype(jnp.bfloat16)]
  transfers between devices with their start and end apart: 3 -> 7, of which waited for: 2 -> 1; matrix products, arithmetic and copies ran while one was open for 20% -> 0% of each run, Pallas kernels for 0% -> 11%
where the time goes in v1:
time: 46.5 us; the launch traced here: 46.4 us
  starting transfers between devices  23.1 us (50%)
  Pallas kernels  16.9 us (36%)
  local copies, waits for them, and re-layouts  3.82 us (8%)
  waiting for transfers between devices  2.33 us (5%)
    all_to_all x1, starting transfers between devices, body(): lax.all_to_all(sums, 'blk', split_axis=0, concat_axis=0, tiled=True)  13 us
    ppermute x6, starting transfers between devices, shifted(): return lax.ppermute(x, 'reg', [(i, (i + d) % NREG) for i in range(NREG)])  10.1 us
    pallas_call x1, Pallas kernels, fill(): pl.pallas_call(fill_kernel, out_shape=jax.ShapeDtypeStruct((NS * NG, 128)...  7.09 us
    pallas_call x1, Pallas kernels, legendre_sums(): pl.pallas_call(legendre_kernel, out_shape=jax.ShapeDtypeStruct((NBLK, 2,...  4.69 us
    pallas_call x1, Pallas kernels, prepare(): pl.pallas_call(prepare_kernel, out_shape=[jax.ShapeDtypeStruct(s, t) for...  3.87 us
    unnamed x30, local copies, waits for them, and re-layouts  3.82 us
    all_to_all x1, waiting for transfers between devices, body(): lax.all_to_all(sums, 'blk', split_axis=0, concat_axis=0, tiled=True)  2.31 us
    pallas_call x1, Pallas kernels, hole_sky(): pl.pallas_call(hole_kernel, out_shape=[jax.ShapeDtypeStruct((HMAX, NS), B...  1.01 us
  transfers between devices with their start and end apart: 7, of which 1 were waited for; matrix products, arithmetic and copies ran while one was open for 0% of the time, Pallas kernels for 11%

profile of v1, /device:TPU:1, one launch (start us, length us, event | category | flops | bytes accessed | tf_op | source)
XLA Modules:
  0.0 46.4 jit_solution(8327280696899347562)
XLA Ops:
  0.0 0.0 copy-start
  0.0 0.0 copy-start.5
  0.0 0.0 copy-start.6
  0.0 0.0 copy-start.7
  0.0 0.0 copy-start.8
  0.0 0.0 copy-start.2
  0.0 4.7 %legendre_sums.1 = bf16[64,2,4,2,128]{4,3,2,1,0:T(2,128)(2,1)} custom-call(bf16[4,64,16,2,128]{4,3,2,1,0:T(2,128)(2,1)} %bitcast.29, bf16[4,2048,256]{2,1,0:T(8,128)(2,1)} %coef.1), custom_call_target="tpu_custom_call" | custom-call | flops 536870912 | bytes 6291456 | tf_op jit(solution)/shard_map/legendre_sums/pallas_call | solution.py:90
  4.7 13.0 %all-to-all-start = ((bf16[64,2,4,2,128]{4,3,2,1,0:T(2,128)(2,1)}), bf16[64,2,4,2,128]{4,3,2,1,0:T(2,128)(2,1)S(1)}, u32[]{:S(2)}, u32[]{:S(2)}) async-start(bf16[64,2,4,2,128]{4,3,2,1,0:T(2,128)(2,1)} %legendre_sums.1), calls=%async_computation | async-start | bytes 524288 | tf_op jit(solution)/shard_map/all_to_all | solution.py:329
  17.7 0.0 copy-done
  17.8 1.4 %collective-permute-start.3 = (bf16[512,256]{1,0:T(8,128)(2,1)S(1)}, bf16[512,256]{1,0:T(8,128)(2,1)S(1)}, u32[]{:S(2)}, u32[]{:S(2)}) collective-permute-start(bf16[512,256]{1,0:T(8,128)(2,1)S(1)} %bitcast.21), channel_id=1, source_target_pairs={{0,1},{1,2},{2,3},{3,0},{4,5},{5,6},{6,7},{7,4},{8,9},{9,10},{10,1... | collective-permute-start | bytes 786440 | tf_op jit(solution)/shard_map/ppermute | solution.py:323
  19.1 2.6 %collective-permute-start.4 = (bf16[512,256]{1,0:T(8,128)(2,1)S(1)}, bf16[512,256]{1,0:T(8,128)(2,1)S(1)}, u32[]{:S(2)}, u32[]{:S(2)}) collective-permute-start(bf16[512,256]{1,0:T(8,128)(2,1)S(1)} %bitcast.22), channel_id=1, source_target_pairs={{0,2},{1,3},{2,0},{3,1},{4,6},{5,7},{6,4},{7,5},{8,10},{9,11},{10,... | collective-permute-start | bytes 786440 | tf_op jit(solution)/shard_map/ppermute | solution.py:323
  21.7 1.1 %collective-permute-start.5 = (bf16[512,256]{1,0:T(8,128)(2,1)S(1)}, bf16[512,256]{1,0:T(8,128)(2,1)S(1)}, u32[]{:S(2)}, u32[]{:S(2)}) collective-permute-start(bf16[512,256]{1,0:T(8,128)(2,1)S(1)} %bitcast.23), channel_id=1, source_target_pairs={{0,3},{1,0},{2,1},{3,2},{4,7},{5,4},{6,5},{7,6},{8,11},{9,8},{10,9... | collective-permute-start | bytes 786440 | tf_op jit(solution)/shard_map/ppermute | solution.py:323
  22.8 0.0 copy-done.5
  22.8 0.0 copy-done.6
  22.8 0.0 copy-done.7
  22.8 0.0 copy-done.8
  22.8 3.9 %prepare.1 = (bf16[256,1024]{1,0:T(8,128)(2,1)S(1)}, bf16[512,1024]{1,0:T(8,128)(2,1)S(1)}, f32[256,128]{1,0:T(8,128)S(1)}, bf16[64,512]{1,0:T(8,128)(2,1)S(1)},...) custom-call(s32[1]{0:T(128)} %bitcast.reg, s32[32,2,128]{2,1,0:T(2,128)S(1)} %bitcast.25, ...), custom_call_target="tpu_custom_call" | custom-call | flops 20000000 | bytes 8388608 | tf_op jit(solution)/shard_map/prepare/pallas_call | solution.py:204
  26.7 0.0 copy-start.9
  26.7 0.6 %copy-done.9 = bf16[512,128]{1,0:T(8,128)(2,1)} copy-done((bf16[512,128]{1,0:T(8,128)(2,1)}, bf16[512,128]{1,0:T(8,128)(2,1)S(1)}, u32[]{:S(2)}) %copy-start.9) | copy-done | bytes 131096
  27.4 0.6 %copy-done.10 = bf16[64,512]{1,0:T(8,128)(2,1)} copy-done((bf16[64,512]{1,0:T(8,128)(2,1)}, bf16[64,512]{1,0:T(8,128)(2,1)S(1)}, u32[]{:S(2)}) %copy-start.10) | copy-done | bytes 65560
  28.0 0.0 copy-start.11
  28.0 0.6 %copy-done.11 = bf16[64,128]{1,0:T(8,128)(2,1)} copy-done((bf16[64,128]{1,0:T(8,128)(2,1)}, bf16[64,128]{1,0:T(8,128)(2,1)S(1)}, u32[]{:S(2)}) %copy-start.11) | copy-done | bytes 16408
  28.6 2.3 %all-to-all-done = bf16[64,2,4,2,128]{4,3,2,1,0:T(2,128)(2,1)S(1)} async-done(((bf16[64,2,4,2,128]{4,3,2,1,0:T(2,128)(2,1)}), bf16[64,2,4,2,128]{4,3,2,1,0:T(2,128)(2,1)S(1)}, u32[]{:S(2)}, u32[]{:S(2)}) %all-to-all-start) | async-done | bytes 262176 | tf_op jit(solution)/shard_map/all_to_all | solution.py:329
  30.9 0.3 residuals.1
  31.2 0.0 copy-start.1
  31.2 1.4 %collective-permute-start = (bf16[64,128]{1,0:T(8,128)(2,1)S(1)}, bf16[64,128]{1,0:T(8,128)(2,1)S(1)}, u32[]{:S(2)}, u32[]{:S(2)}) collective-permute-start(bf16[64,128]{1,0:T(8,128)(2,1)S(1)} %get-tuple-element.20), channel_id=1, source_target_pairs={{0,1},{1,2},{2,3},{3,0},{4,5},{5,6},{6,7},{7,4},{8,9},{9,10},{10,1... | collective-permute-start | bytes 49160 | tf_op jit(solution)/shard_map/ppermute | solution.py:323
  32.6 2.6 %collective-permute-start.1 = (bf16[64,128]{1,0:T(8,128)(2,1)S(1)}, bf16[64,128]{1,0:T(8,128)(2,1)S(1)}, u32[]{:S(2)}, u32[]{:S(2)}) collective-permute-start(bf16[64,128]{1,0:T(8,128)(2,1)S(1)} %get-tuple-element.21), channel_id=1, source_target_pairs={{0,2},{1,3},{2,0},{3,1},{4,6},{5,7},{6,4},{7,5},{8,10},{9,11},{10,... | collective-permute-start | bytes 49160 | tf_op jit(solution)/shard_map/ppermute | solution.py:323
  35.2 0.0 collective-permute-done.3.tile1
  35.2 1.1 %collective-permute-start.2 = (bf16[64,128]{1,0:T(8,128)(2,1)S(1)}, bf16[64,128]{1,0:T(8,128)(2,1)S(1)}, u32[]{:S(2)}, u32[]{:S(2)}) collective-permute-start(bf16[64,128]{1,0:T(8,128)(2,1)S(1)} %get-tuple-element.22), channel_id=1, source_target_pairs={{0,3},{1,0},{2,1},{3,2},{4,7},{5,4},{6,5},{7,6},{8,11},{9,8},{10,9... | collective-permute-start | bytes 49160 | tf_op jit(solution)/shard_map/ppermute | solution.py:323
  36.3 0.0 collective-permute-done.4.tile2
  36.3 0.0 collective-permute-done.5.tile3
  36.3 0.0 copy-done.2
  36.3 1.0 %hole_sky.1 = (bf16[512,128]{1,0:T(8,128)(2,1)S(1)}, bf16[512,256]{1,0:T(8,128)(2,1)S(1)}) custom-call(s32[1]{0:T(128)} %bitcast.reg, s32[1,4]{1,0:T(1,128)S(1)} %copy-done.2, bf16[1024,128]{1,0:T(8,128)(2,1)S(1)} %bitcast.20, bf16[512,1024]{1,0:T(8,128)(2,1)S(1)} %get-tuple-element.23.ph, bf16[512,256]{1,0:T(8,128)(2,1)S(1)} %bitcast.24, ...), custom_call_target="tpu_custom_call" | custom-call | flops 134217728 | bytes 2097152 | tf_op jit(solution)/shard_map/hole_sky/pallas_call | solution.py:254
  37.3 0.0 copy-start.3
  37.3 0.7 %copy-done.3 = bf16[512,256]{1,0:T(8,128)(2,1)} copy-done((bf16[512,256]{1,0:T(8,128)(2,1)}, bf16[512,256]{1,0:T(8,128)(2,1)S(1)}, u32[]{:S(2)}) %copy-start.3) | copy-done | bytes 262168
  38.0 0.0 copy-start.4
  38.0 0.6 %copy-done.4 = bf16[512,128]{1,0:T(8,128)(2,1)} copy-done((bf16[512,128]{1,0:T(8,128)(2,1)}, bf16[512,128]{1,0:T(8,128)(2,1)S(1)}, u32[]{:S(2)}) %copy-start.4) | copy-done | bytes 131096
  38.6 0.0 collective-permute-done.from1
  38.7 0.0 copy-start.12
  38.7 0.0 collective-permute-done.1.from2
  38.7 0.0 copy-start.13
  38.7 0.0 collective-permute-done.2.from3
  38.7 0.0 copy-start.14
  38.7 0.0 copy-done.1
  38.7 0.5 %copy-done.12 = bf16[64,128]{1,0:T(8,128)(2,1)} copy-done((bf16[64,128]{1,0:T(8,128)(2,1)}, bf16[64,128]{1,0:T(8,128)(2,1)S(1)}, u32[]{:S(2)}) %copy-start.12) | copy-done | bytes 16408
  39.2 0.0 copy-done.13
  39.3 0.0 copy-done.14
  39.3 7.1 %fill.1 = bf16[8192,128]{1,0:T(8,128)(2,1)} custom-call(s32[1]{0:T(128)} %bitcast.reg, bf16[64,128]{1,0:T(8,128)(2,1)} %copy-done.1, bf16[64,128]{1,0:T(8,128)(2,1)} %copy-done.12, bf16[64,128]{1,0:T(8,128)(2,1)} %copy-done.13, bf16[64,128]{1,0:T(8,128)(2,1)} %copy-done.14, bf16[512,256]{1,0:T(8,128)(2,1)} %copy-done.3, bf16[512,128]{1,0:T(8,128)(2,1)} %copy-done.4, ...), custom_call_target="tpu_custom_call" | custom-call | flops 1073741824 | bytes 3145728 | tf_op jit(solution)/shard_map/fill/pallas_call | solution.py:301
  (1 shorter events, 0.0 us)
Async XLA Ops:
  0.0 17.7 %copy-start = (bf16[1,1,512,256]{3,2,1,0:T(8,128)(2,1)S(1)}, bf16[1,1,512,256]{3,2,1,0:T(8,128)(2,1)}, u32[]{:S(2)}) copy-start(bf16[1,1,512,256]{3,2,1,0:T(8,128)(2,1)} %param.15) | copy-start | bytes 786436
  0.0 22.8 %copy-start.5 = (s32[2,4096]{1,0:T(2,128)S(1)}, s32[2,4096]{1,0:T(2,128)}, u32[]{:S(2)}) copy-start(s32[2,4096]{1,0:T(2,128)} %param.12) | copy-start | bytes 98308
  0.0 22.8 %copy-start.6 = (f32[2,4096]{1,0:T(2,128)S(1)}, f32[2,4096]{1,0:T(2,128)}, u32[]{:S(2)}) copy-start(f32[2,4096]{1,0:T(2,128)} %param.11) | copy-start | bytes 98308
  0.0 22.8 %copy-start.7 = (s32[1,4,256]{2,1,0:T(4,128)S(1)}, s32[1,4,256]{2,1,0:T(4,128)}, u32[]{:S(2)}) copy-start(s32[1,4,256]{2,1,0:T(4,128)} %param.13) | copy-start | bytes 12292
  0.0 22.8 %copy-start.8 = (s32[256]{0:T(256)S(1)}, s32[256]{0:T(256)}, u32[]{:S(2)}) copy-start(s32[256]{0:T(256)} %param.10) | copy-start | bytes 3076
  0.0 36.3 %copy-start.2 = (s32[1,4]{1,0:T(1,128)S(1)}, s32[1,4]{1,0:T(1,128)}, u32[]{:S(2)}) copy-start(s32[1,4]{1,0:T(1,128)} %owners.1) | copy-start | bytes 52
  4.7 26.2 %all-to-all-start = ((bf16[64,2,4,2,128]{4,3,2,1,0:T(2,128)(2,1)}), bf16[64,2,4,2,128]{4,3,2,1,0:T(2,128)(2,1)S(1)}, u32[]{:S(2)}, u32[]{:S(2)}) async-start(bf16[64,2,4,2,128]{4,3,2,1,0:T(2,128)(2,1)} %legendre_sums.1), calls=%async_computation | async-start | bytes 524288 | tf_op jit(solution)/shard_map/all_to_all | solution.py:329
  17.8 17.5 %collective-permute-start.3 = (bf16[512,256]{1,0:T(8,128)(2,1)S(1)}, bf16[512,256]{1,0:T(8,128)(2,1)S(1)}, u32[]{:S(2)}, u32[]{:S(2)}) collective-permute-start(bf16[512,256]{1,0:T(8,128)(2,1)S(1)} %bitcast.21), channel_id=1, source_target_pairs={{0,1},{1,2},{2,3},{3,0},{4,5},{5,6},{6,7},{7,4},{8,9},{9,10},{10,1... | collective-permute-start | bytes 786440 | tf_op jit(solution)/shard_map/ppermute | solution.py:323
  19.1 17.2 %collective-permute-start.4 = (bf16[512,256]{1,0:T(8,128)(2,1)S(1)}, bf16[512,256]{1,0:T(8,128)(2,1)S(1)}, u32[]{:S(2)}, u32[]{:S(2)}) collective-permute-start(bf16[512,256]{1,0:T(8,128)(2,1)S(1)} %bitcast.22), channel_id=1, source_target_pairs={{0,2},{1,3},{2,0},{3,1},{4,6},{5,7},{6,4},{7,5},{8,10},{9,11},{10,... | collective-permute-start | bytes 786440 | tf_op jit(solution)/shard_map/ppermute | solution.py:323
  21.7 14.5 %collective-permute-start.5 = (bf16[512,256]{1,0:T(8,128)(2,1)S(1)}, bf16[512,256]{1,0:T(8,128)(2,1)S(1)}, u32[]{:S(2)}, u32[]{:S(2)}) collective-permute-start(bf16[512,256]{1,0:T(8,128)(2,1)S(1)} %bitcast.23), channel_id=1, source_target_pairs={{0,3},{1,0},{2,1},{3,2},{4,7},{5,4},{6,5},{7,6},{8,11},{9,8},{10,9... | collective-permute-start | bytes 786440 | tf_op jit(solution)/shard_map/ppermute | solution.py:323
  26.7 0.7 %copy-start.9 = (bf16[512,128]{1,0:T(8,128)(2,1)}, bf16[512,128]{1,0:T(8,128)(2,1)S(1)}, u32[]{:S(2)}) copy-start(bf16[512,128]{1,0:T(8,128)(2,1)S(1)} %get-tuple-element.27.lan) | copy-start | bytes 393220
  27.4 0.6 %copy-start.10 = (bf16[64,512]{1,0:T(8,128)(2,1)}, bf16[64,512]{1,0:T(8,128)(2,1)S(1)}, u32[]{:S(2)}) copy-start(bf16[64,512]{1,0:T(8,128)(2,1)S(1)} %get-tuple-element.26.grp) | copy-start | bytes 196612
  28.0 0.6 %copy-start.11 = (bf16[64,128]{1,0:T(8,128)(2,1)}, bf16[64,128]{1,0:T(8,128)(2,1)S(1)}, u32[]{:S(2)}) copy-start(bf16[64,128]{1,0:T(8,128)(2,1)S(1)} %get-tuple-element.28.obsm) | copy-start | bytes 49156
  31.2 7.5 %copy-start.1 = (bf16[64,128]{1,0:T(8,128)(2,1)}, bf16[64,128]{1,0:T(8,128)(2,1)S(1)}, u32[]{:S(2)}) copy-start(bf16[64,128]{1,0:T(8,128)(2,1)S(1)} %get-tuple-element.19.after.own) | copy-start | bytes 49156
  31.2 7.4 %collective-permute-start = (bf16[64,128]{1,0:T(8,128)(2,1)S(1)}, bf16[64,128]{1,0:T(8,128)(2,1)S(1)}, u32[]{:S(2)}, u32[]{:S(2)}) collective-permute-start(bf16[64,128]{1,0:T(8,128)(2,1)S(1)} %get-tuple-element.20), channel_id=1, source_target_pairs={{0,1},{1,2},{2,3},{3,0},{4,5},{5,6},{6,7},{7,4},{8,9},{9,10},{10,1... | collective-permute-start | bytes 49160 | tf_op jit(solution)/shard_map/ppermute | solution.py:323
  32.6 6.1 %collective-permute-start.1 = (bf16[64,128]{1,0:T(8,128)(2,1)S(1)}, bf16[64,128]{1,0:T(8,128)(2,1)S(1)}, u32[]{:S(2)}, u32[]{:S(2)}) collective-permute-start(bf16[64,128]{1,0:T(8,128)(2,1)S(1)} %get-tuple-element.21), channel_id=1, source_target_pairs={{0,2},{1,3},{2,0},{3,1},{4,6},{5,7},{6,4},{7,5},{8,10},{9,11},{10,... | collective-permute-start | bytes 49160 | tf_op jit(solution)/shard_map/ppermute | solution.py:323
  35.2 3.5 %collective-permute-start.2 = (bf16[64,128]{1,0:T(8,128)(2,1)S(1)}, bf16[64,128]{1,0:T(8,128)(2,1)S(1)}, u32[]{:S(2)}, u32[]{:S(2)}) collective-permute-start(bf16[64,128]{1,0:T(8,128)(2,1)S(1)} %get-tuple-element.22), channel_id=1, source_target_pairs={{0,3},{1,0},{2,1},{3,2},{4,7},{5,4},{6,5},{7,6},{8,11},{9,8},{10,9... | collective-permute-start | bytes 49160 | tf_op jit(solution)/shard_map/ppermute | solution.py:323
  37.3 0.7 %copy-start.3 = (bf16[512,256]{1,0:T(8,128)(2,1)}, bf16[512,256]{1,0:T(8,128)(2,1)S(1)}, u32[]{:S(2)}) copy-start(bf16[512,256]{1,0:T(8,128)(2,1)S(1)} %get-tuple-element.24.tile) | copy-start | bytes 786436
  38.0 0.6 %copy-start.4 = (bf16[512,128]{1,0:T(8,128)(2,1)}, bf16[512,128]{1,0:T(8,128)(2,1)S(1)}, u32[]{:S(2)}) copy-start(bf16[512,128]{1,0:T(8,128)(2,1)S(1)} %get-tuple-element.25.sky) | copy-start | bytes 393220
  38.7 0.6 %copy-start.12 = (bf16[64,128]{1,0:T(8,128)(2,1)}, bf16[64,128]{1,0:T(8,128)(2,1)S(1)}, u32[]{:S(2)}) copy-start(bf16[64,128]{1,0:T(8,128)(2,1)S(1)} %collective-permute-done.from1) | copy-start | bytes 49156
  38.7 0.6 %copy-start.13 = (bf16[64,128]{1,0:T(8,128)(2,1)}, bf16[64,128]{1,0:T(8,128)(2,1)S(1)}, u32[]{:S(2)}) copy-start(bf16[64,128]{1,0:T(8,128)(2,1)S(1)} %collective-permute-done.1.from2) | copy-start | bytes 49156
  38.7 0.6 %copy-start.14 = (bf16[64,128]{1,0:T(8,128)(2,1)}, bf16[64,128]{1,0:T(8,128)(2,1)S(1)}, u32[]{:S(2)}) copy-start(bf16[64,128]{1,0:T(8,128)(2,1)S(1)} %collective-permute-done.2.from3) | copy-start | bytes 49156

commit v2 on v1

--- a/solution.py
+++ b/solution.py
@@ -16,7 +16,8 @@
 L = 2048
 KT = L // 128
 NPHI = 4096
-NG = 2 * NPHI // 128
+NT = NPHI // 128
+NG = 2 * NT
 NB = 256
 SLOTS = NB // NREG
 HMAX = 512
@@ -129,10 +130,11 @@
     pick_t = (iota((32, HMAX), 1) // 16 == iota((32, HMAX), 0)).astype(F32).astype(BF)
     low_t = iota((16, HMAX), 1) % 16 == iota((16, HMAX), 0)
     g1_row = jnp.sum(jnp.where(low_t, dot(wide[:, 0:32], pick_t), 0.0), axis=0, keepdims=True)
-    grp[...] = jnp.where((iota((NG, HMAX), 0) + 1).astype(F32) == g1_row, 1.0, 0.0).astype(BF)
-    lan[...] = jnp.where(iota((HMAX, 128), 1).astype(F32) == lh, 1.0, 0.0).astype(BF)
+    grp[...] = jnp.where(iota((NT, HMAX), 0).astype(F32) == jnp.floor((g1_row - 1.0) * 0.5), 1.0, 0.0).astype(BF)
     gh = g1 - 1.0
     tile_h = jnp.floor(gh * 0.5)
+    place = (gh - 2.0 * tile_h) * 128.0 + lh
+    lan[...] = jnp.where(iota((HMAX, 256), 1).astype(F32) == place, 1.0, 0.0).astype(BF)
     pcol[NB:, :] = jnp.broadcast_to(tile_h * 128.0 + lh, (HMAX, 128))
     rcol[NB:, :] = jnp.broadcast_to(gh - 2.0 * tile_h, (HMAX, 128))
 
@@ -197,8 +199,8 @@
         ((NB, NK), BF),
         ((HMAX, NK), BF),
         ((NB, 128), F32),
-        ((NG, HMAX), BF),
-        ((HMAX, 128), BF),
+        ((NT, HMAX), BF),
+        ((HMAX, 256), BF),
         ((NG, 128), BF),
     ]
     return pl.pallas_call(
@@ -278,22 +280,17 @@
     base = obsm[...]
 
     def copy(i):
-        at = pl.ds(pl.multiple_of(i * (CHUNK * NG), CHUNK * NG), CHUNK * NG)
+        at = pl.ds(i * CHUNK * NG, CHUNK * NG)
         return pltpu.make_async_copy(outv.at[at], out.at[at], sem)
 
-    def step(i, _):
-        parts = []
+    for i in range(NS // CHUNK):
+        parts = [groups * xt[i * CHUNK + j : i * CHUNK + j + 1, :].astype(BF) for j in range(CHUNK)]
+        got = dot(jnp.concatenate(parts, axis=0), lanes)
+        got = got.reshape(CHUNK * NG, 128).astype(BF)
         for j in range(CHUNK):
-            line = xt[pl.ds(i * CHUNK + j, 1), :].astype(BF)
-            parts.append(groups * line)
-        got = dot(jnp.concatenate(parts, axis=0), lanes).astype(BF)
-        for j in range(CHUNK):
-            at = pl.multiple_of(i * (CHUNK * NG) + j * NG, NG)
-            outv[pl.ds(at, NG), :] = got[j * NG : (j + 1) * NG] + base
+            at = i * CHUNK * NG + j * NG
+            outv[at : at + NG, :] = got[j * NG : (j + 1) * NG, :] + base
         copy(i).start()
-        return 0
-
-    lax.fori_loop(0, NS // CHUNK, step, 0)
     pltpu.make_async_copy(outv, outv, sem).wait()
 
 
@@ -309,7 +306,7 @@
             pltpu.VMEM((NS * NG, 128), BF),
             pltpu.SemaphoreType.DMA,
         ],
-        compiler_params=params(60),
+        compiler_params=params(16),
         cost_estimate=pl.CostEstimate(flops=2 * NS * NG * HMAX * 128, bytes_accessed=3 * MB, transcendentals=0),
         name="fill",
     )(reg, *edges, tile, sky, grp, lan, obsm)

time: 46.5 us -> 40.5 us (0.87)
  Pallas kernels: 16.9 us -> 12.2 us
  local copies, waits for them, and re-layouts: 3.82 us -> 0.02 us
  waiting for transfers between devices: 2.33 us -> 4.86 us
    pallas_call x1, Pallas kernels: 7.09 us -> 2.39 us  [fill(): pl.pallas_call(fill_kernel, out_shape=jax.ShapeDtypeStruct((NS * NG, 128)...]
    unnamed x30 -> x12, local copies, waits for them, and re-layouts: 3.82 us -> 0.02 us
    all_to_all x1, waiting for transfers between devices: 2.31 us -> 4.19 us  [body(): lax.all_to_all(sums, 'blk', split_axis=0, concat_axis=0, tiled=True)]
    ppermute x6, waiting for transfers between devices: 0.02 us -> 0.66 us  [shifted(): return lax.ppermute(x, 'reg', [(i, (i + d) % NREG) for i in range(NREG)])]
  transfers between devices with their start and end apart: 7 -> 7, of which waited for: 1 -> 2; matrix products, arithmetic and copies ran while one was open for 0% -> 0% of each run, Pallas kernels for 11% -> 13%
where the time goes in v2:
time: 40.5 us; the launch traced here: 40.3 us
  starting transfers between devices  23.1 us (57%)
  Pallas kernels  12.2 us (30%)
  waiting for transfers between devices  4.86 us (12%)
    all_to_all x1, starting transfers between devices, body(): lax.all_to_all(sums, 'blk', split_axis=0, concat_axis=0, tiled=True)  13 us
    ppermute x6, starting transfers between devices, shifted(): return lax.ppermute(x, 'reg', [(i, (i + d) % NREG) for i in range(NREG)])  10.1 us
    pallas_call x1, Pallas kernels, legendre_sums(): pl.pallas_call(legendre_kernel, out_shape=jax.ShapeDtypeStruct((NBLK, 2,...  4.69 us
    all_to_all x1, waiting for transfers between devices, body(): lax.all_to_all(sums, 'blk', split_axis=0, concat_axis=0, tiled=True)  4.19 us
    pallas_call x1, Pallas kernels, prepare(): pl.pallas_call(prepare_kernel, out_shape=[jax.ShapeDtypeStruct(s, t) for...  3.87 us
    pallas_call x1, Pallas kernels, fill(): pl.pallas_call(fill_kernel, out_shape=jax.ShapeDtypeStruct((NS * NG, 128)...  2.39 us
    pallas_call x1, Pallas kernels, hole_sky(): pl.pallas_call(hole_kernel, out_shape=[jax.ShapeDtypeStruct((HMAX, NS), B...  1 us
  transfers between devices with their start and end apart: 7, of which 2 were waited for; matrix products, arithmetic and copies ran while one was open for 0% of the time, Pallas kernels for 13%

profile of v2, /device:TPU:1, one launch (start us, length us, event | category | flops | bytes accessed | tf_op | source)
XLA Modules:
  0.0 40.3 jit_solution(6294297763141824729)
XLA Ops:
  0.0 0.0 copy-start
  0.0 0.0 copy-start.2
  0.0 0.0 copy-start.3
  0.0 0.0 copy-start.4
  0.0 0.0 copy-start.5
  0.0 0.0 copy-start.1
  0.0 4.7 %legendre_sums.1 = bf16[64,2,4,2,128]{4,3,2,1,0:T(2,128)(2,1)} custom-call(bf16[4,64,16,2,128]{4,3,2,1,0:T(2,128)(2,1)} %bitcast.29, bf16[4,2048,256]{2,1,0:T(8,128)(2,1)} %coef.1), custom_call_target="tpu_custom_call" | custom-call | flops 536870912 | bytes 6291456 | tf_op jit(solution)/shard_map/legendre_sums/pallas_call | solution.py:91
  4.7 13.0 %all-to-all-start = ((bf16[64,2,4,2,128]{4,3,2,1,0:T(2,128)(2,1)}), bf16[64,2,4,2,128]{4,3,2,1,0:T(2,128)(2,1)S(1)}, u32[]{:S(2)}, u32[]{:S(2)}) async-start(bf16[64,2,4,2,128]{4,3,2,1,0:T(2,128)(2,1)} %legendre_sums.1), calls=%async_computation | async-start | bytes 524288 | tf_op jit(solution)/shard_map/all_to_all | solution.py:326
  17.7 0.0 copy-done
  17.8 1.4 %collective-permute-start.3 = (bf16[512,256]{1,0:T(8,128)(2,1)S(1)}, bf16[512,256]{1,0:T(8,128)(2,1)S(1)}, u32[]{:S(2)}, u32[]{:S(2)}) collective-permute-start(bf16[512,256]{1,0:T(8,128)(2,1)S(1)} %bitcast.21), channel_id=1, source_target_pairs={{0,1},{1,2},{2,3},{3,0},{4,5},{5,6},{6,7},{7,4},{8,9},{9,10},{10,1... | collective-permute-start | bytes 786440 | tf_op jit(solution)/shard_map/ppermute | solution.py:320
  19.1 2.6 %collective-permute-start.4 = (bf16[512,256]{1,0:T(8,128)(2,1)S(1)}, bf16[512,256]{1,0:T(8,128)(2,1)S(1)}, u32[]{:S(2)}, u32[]{:S(2)}) collective-permute-start(bf16[512,256]{1,0:T(8,128)(2,1)S(1)} %bitcast.22), channel_id=1, source_target_pairs={{0,2},{1,3},{2,0},{3,1},{4,6},{5,7},{6,4},{7,5},{8,10},{9,11},{10,... | collective-permute-start | bytes 786440 | tf_op jit(solution)/shard_map/ppermute | solution.py:320
  21.7 1.1 %collective-permute-start.5 = (bf16[512,256]{1,0:T(8,128)(2,1)S(1)}, bf16[512,256]{1,0:T(8,128)(2,1)S(1)}, u32[]{:S(2)}, u32[]{:S(2)}) collective-permute-start(bf16[512,256]{1,0:T(8,128)(2,1)S(1)} %bitcast.23), channel_id=1, source_target_pairs={{0,3},{1,0},{2,1},{3,2},{4,7},{5,4},{6,5},{7,6},{8,11},{9,8},{10,9... | collective-permute-start | bytes 786440 | tf_op jit(solution)/shard_map/ppermute | solution.py:320
  22.8 0.0 copy-done.2
  22.8 0.0 copy-done.3
  22.8 0.0 copy-done.4
  22.8 0.0 copy-done.5
  22.8 3.9 %prepare.1 = (bf16[256,1024]{1,0:T(8,128)(2,1)S(1)}, bf16[512,1024]{1,0:T(8,128)(2,1)S(1)}, f32[256,128]{1,0:T(8,128)S(1)}, bf16[32,512]{1,0:T(8,128)(2,1)S(1)},...) custom-call(s32[1]{0:T(128)} %bitcast.reg, s32[32,2,128]{2,1,0:T(2,128)S(1)} %bitcast.25, ...), custom_call_target="tpu_custom_call" | custom-call | flops 20000000 | bytes 8388608 | tf_op jit(solution)/shard_map/prepare/pallas_call | solution.py:206
  26.7 4.2 %all-to-all-done = bf16[64,2,4,2,128]{4,3,2,1,0:T(2,128)(2,1)S(1)} async-done(((bf16[64,2,4,2,128]{4,3,2,1,0:T(2,128)(2,1)}), bf16[64,2,4,2,128]{4,3,2,1,0:T(2,128)(2,1)S(1)}, u32[]{:S(2)}, u32[]{:S(2)}) %all-to-all-start) | async-done | bytes 262176 | tf_op jit(solution)/shard_map/all_to_all | solution.py:326
  30.9 0.3 residuals.1
  31.2 1.4 %collective-permute-start = (bf16[64,128]{1,0:T(8,128)(2,1)S(1)}, bf16[64,128]{1,0:T(8,128)(2,1)S(1)}, u32[]{:S(2)}, u32[]{:S(2)}) collective-permute-start(bf16[64,128]{1,0:T(8,128)(2,1)S(1)} %get-tuple-element.20), channel_id=1, source_target_pairs={{0,1},{1,2},{2,3},{3,0},{4,5},{5,6},{6,7},{7,4},{8,9},{9,10},{10,1... | collective-permute-start | bytes 49160 | tf_op jit(solution)/shard_map/ppermute | solution.py:320
  32.6 2.6 %collective-permute-start.1 = (bf16[64,128]{1,0:T(8,128)(2,1)S(1)}, bf16[64,128]{1,0:T(8,128)(2,1)S(1)}, u32[]{:S(2)}, u32[]{:S(2)}) collective-permute-start(bf16[64,128]{1,0:T(8,128)(2,1)S(1)} %get-tuple-element.21), channel_id=1, source_target_pairs={{0,2},{1,3},{2,0},{3,1},{4,6},{5,7},{6,4},{7,5},{8,10},{9,11},{10,... | collective-permute-start | bytes 49160 | tf_op jit(solution)/shard_map/ppermute | solution.py:320
  35.2 0.0 collective-permute-done.3.tile1
  35.2 1.1 %collective-permute-start.2 = (bf16[64,128]{1,0:T(8,128)(2,1)S(1)}, bf16[64,128]{1,0:T(8,128)(2,1)S(1)}, u32[]{:S(2)}, u32[]{:S(2)}) collective-permute-start(bf16[64,128]{1,0:T(8,128)(2,1)S(1)} %get-tuple-element.22), channel_id=1, source_target_pairs={{0,3},{1,0},{2,1},{3,2},{4,7},{5,4},{6,5},{7,6},{8,11},{9,8},{10,9... | collective-permute-start | bytes 49160 | tf_op jit(solution)/shard_map/ppermute | solution.py:320
  36.3 0.0 collective-permute-done.4.tile2
  36.3 0.0 collective-permute-done.5.tile3
  36.3 0.0 copy-done.1
  36.3 1.0 %hole_sky.1 = (bf16[512,128]{1,0:T(8,128)(2,1)S(1)}, bf16[512,256]{1,0:T(8,128)(2,1)S(1)}) custom-call(s32[1]{0:T(128)} %bitcast.reg, s32[1,4]{1,0:T(1,128)S(1)} %copy-done.1, bf16[1024,128]{1,0:T(8,128)(2,1)S(1)} %bitcast.20, bf16[512,1024]{1,0:T(8,128)(2,1)S(1)} %get-tuple-element.23.ph, bf16[512,256]{1,0:T(8,128)(2,1)S(1)} %bitcast.24, ...), custom_call_target="tpu_custom_call" | custom-call | flops 134217728 | bytes 2097152 | tf_op jit(solution)/shard_map/hole_sky/pallas_call | solution.py:256
  37.3 0.0 collective-permute-done.from1
  37.3 0.0 collective-permute-done.1.from2
  37.3 0.6 %collective-permute-done.2.from3 = bf16[64,128]{1,0:T(8,128)(2,1)S(1)} collective-permute-done((bf16[64,128]{1,0:T(8,128)(2,1)S(1)}, bf16[64,128]{1,0:T(8,128)(2,1)S(1)}, u32[]{:S(2)}, u32[]{:S(2)}) %collective-permute-start.2) | collective-permute-done | bytes 16416 | tf_op jit(solution)/shard_map/ppermute | solution.py:320
  38.0 2.4 %fill.1 = bf16[8192,128]{1,0:T(8,128)(2,1)} custom-call(s32[1]{0:T(128)} %bitcast.reg, bf16[64,128]{1,0:T(8,128)(2,1)S(1)} %get-tuple-element.19.after.own, bf16[64,128]{1,0:T(8,128)(2,1)S(1)} %collective-permute-done.from1, bf16[64,128]{1,0:T(8,128)(2,1)S(1)} %collective-permute-done.1.from2, bf16[64,128]{1,0:T(8,128)(2,1)S(1)} %collective-permute-done.2.from3, ...), custom_call_target="tpu_custom_call" | custom-call | flops 1073741824 | bytes 3145728 | tf_op jit(solution)/shard_map/fill/pallas_call | solution.py:298
Async XLA Ops:
  0.0 17.7 %copy-start = (bf16[1,1,512,256]{3,2,1,0:T(8,128)(2,1)S(1)}, bf16[1,1,512,256]{3,2,1,0:T(8,128)(2,1)}, u32[]{:S(2)}) copy-start(bf16[1,1,512,256]{3,2,1,0:T(8,128)(2,1)} %param.15) | copy-start | bytes 786436
  0.0 22.8 %copy-start.2 = (s32[2,4096]{1,0:T(2,128)S(1)}, s32[2,4096]{1,0:T(2,128)}, u32[]{:S(2)}) copy-start(s32[2,4096]{1,0:T(2,128)} %param.12) | copy-start | bytes 98308
  0.0 22.8 %copy-start.3 = (f32[2,4096]{1,0:T(2,128)S(1)}, f32[2,4096]{1,0:T(2,128)}, u32[]{:S(2)}) copy-start(f32[2,4096]{1,0:T(2,128)} %param.11) | copy-start | bytes 98308
  0.0 22.8 %copy-start.4 = (s32[1,4,256]{2,1,0:T(4,128)S(1)}, s32[1,4,256]{2,1,0:T(4,128)}, u32[]{:S(2)}) copy-start(s32[1,4,256]{2,1,0:T(4,128)} %param.13) | copy-start | bytes 12292
  0.0 22.8 %copy-start.5 = (s32[256]{0:T(256)S(1)}, s32[256]{0:T(256)}, u32[]{:S(2)}) copy-start(s32[256]{0:T(256)} %param.10) | copy-start | bytes 3076
  0.0 36.2 %copy-start.1 = (s32[1,4]{1,0:T(1,128)S(1)}, s32[1,4]{1,0:T(1,128)}, u32[]{:S(2)}) copy-start(s32[1,4]{1,0:T(1,128)} %owners.1) | copy-start | bytes 52
  4.7 26.2 %all-to-all-start = ((bf16[64,2,4,2,128]{4,3,2,1,0:T(2,128)(2,1)}), bf16[64,2,4,2,128]{4,3,2,1,0:T(2,128)(2,1)S(1)}, u32[]{:S(2)}, u32[]{:S(2)}) async-start(bf16[64,2,4,2,128]{4,3,2,1,0:T(2,128)(2,1)} %legendre_sums.1), calls=%async_computation | async-start | bytes 524288 | tf_op jit(solution)/shard_map/all_to_all | solution.py:326
  17.8 17.4 %collective-permute-start.3 = (bf16[512,256]{1,0:T(8,128)(2,1)S(1)}, bf16[512,256]{1,0:T(8,128)(2,1)S(1)}, u32[]{:S(2)}, u32[]{:S(2)}) collective-permute-start(bf16[512,256]{1,0:T(8,128)(2,1)S(1)} %bitcast.21), channel_id=1, source_target_pairs={{0,1},{1,2},{2,3},{3,0},{4,5},{5,6},{6,7},{7,4},{8,9},{9,10},{10,1... | collective-permute-start | bytes 786440 | tf_op jit(solution)/shard_map/ppermute | solution.py:320
  19.1 17.1 %collective-permute-start.4 = (bf16[512,256]{1,0:T(8,128)(2,1)S(1)}, bf16[512,256]{1,0:T(8,128)(2,1)S(1)}, u32[]{:S(2)}, u32[]{:S(2)}) collective-permute-start(bf16[512,256]{1,0:T(8,128)(2,1)S(1)} %bitcast.22), channel_id=1, source_target_pairs={{0,2},{1,3},{2,0},{3,1},{4,6},{5,7},{6,4},{7,5},{8,10},{9,11},{10,... | collective-permute-start | bytes 786440 | tf_op jit(solution)/shard_map/ppermute | solution.py:320
  21.7 14.5 %collective-permute-start.5 = (bf16[512,256]{1,0:T(8,128)(2,1)S(1)}, bf16[512,256]{1,0:T(8,128)(2,1)S(1)}, u32[]{:S(2)}, u32[]{:S(2)}) collective-permute-start(bf16[512,256]{1,0:T(8,128)(2,1)S(1)} %bitcast.23), channel_id=1, source_target_pairs={{0,3},{1,0},{2,1},{3,2},{4,7},{5,4},{6,5},{7,6},{8,11},{9,8},{10,9... | collective-permute-start | bytes 786440 | tf_op jit(solution)/shard_map/ppermute | solution.py:320
  31.2 6.1 %collective-permute-start = (bf16[64,128]{1,0:T(8,128)(2,1)S(1)}, bf16[64,128]{1,0:T(8,128)(2,1)S(1)}, u32[]{:S(2)}, u32[]{:S(2)}) collective-permute-start(bf16[64,128]{1,0:T(8,128)(2,1)S(1)} %get-tuple-element.20), channel_id=1, source_target_pairs={{0,1},{1,2},{2,3},{3,0},{4,5},{5,6},{6,7},{7,4},{8,9},{9,10},{10,1... | collective-permute-start | bytes 49160 | tf_op jit(solution)/shard_map/ppermute | solution.py:320
  32.6 4.7 %collective-permute-start.1 = (bf16[64,128]{1,0:T(8,128)(2,1)S(1)}, bf16[64,128]{1,0:T(8,128)(2,1)S(1)}, u32[]{:S(2)}, u32[]{:S(2)}) collective-permute-start(bf16[64,128]{1,0:T(8,128)(2,1)S(1)} %get-tuple-element.21), channel_id=1, source_target_pairs={{0,2},{1,3},{2,0},{3,1},{4,6},{5,7},{6,4},{7,5},{8,10},{9,11},{10,... | collective-permute-start | bytes 49160 | tf_op jit(solution)/shard_map/ppermute | solution.py:320
  35.2 2.8 %collective-permute-start.2 = (bf16[64,128]{1,0:T(8,128)(2,1)S(1)}, bf16[64,128]{1,0:T(8,128)(2,1)S(1)}, u32[]{:S(2)}, u32[]{:S(2)}) collective-permute-start(bf16[64,128]{1,0:T(8,128)(2,1)S(1)} %get-tuple-element.22), channel_id=1, source_target_pairs={{0,3},{1,0},{2,1},{3,2},{4,7},{5,4},{6,5},{7,6},{8,11},{9,8},{10,9... | collective-permute-start | bytes 49160 | tf_op jit(solution)/shard_map/ppermute | solution.py:320

commit v3 on v2

--- a/solution.py
+++ b/solution.py
@@ -64,26 +64,32 @@
     return lax.dot_general(a, b, (((1,), (1,)), ((), ())), preferred_element_type=F32)
 
 
-def legendre_kernel(leg, coef, out, legv, coefv, resv, lsem, csem, osem):
-    def coef_copy(m):
-        return pltpu.make_async_copy(coef.at[m], coefv.at[m], csem.at[m])
-
+STEPS = 8
+WIDE = KT // STEPS
+DEEP = L // STEPS
+
+
+def legendre_kernel(leg, coef, out, legv, coefv, lsem, csem):
+    def coef_copy(k):
+        at = pl.ds(k * DEEP, DEEP)
+        return pltpu.make_async_copy(coef.at[:, at], coefv.at[:, at], csem.at[k])
+
+    for k in range(STEPS):
+        for t in range(k * WIDE, (k + 1) * WIDE):
+            pltpu.make_async_copy(leg.at[:, :, t], legv.at[t], lsem.at[k]).start()
+        coef_copy(k).start()
+    totals = [jnp.zeros((2 * NBLK, 2 * NS), F32)] * NM
+    for k in range(STEPS):
+        part = legv.at[k * WIDE : (k + 1) * WIDE]
+        pltpu.make_async_copy(part, part, lsem.at[k]).wait()
+        coef_copy(k).wait()
+        for m in range(NM):
+            left = [legv.at[t, m].reshape(2 * NBLK, 128)[...] for t in range(k * WIDE, (k + 1) * WIDE)]
+            totals[m] += dot(jnp.concatenate(left, axis=1), coefv[m, k * DEEP : (k + 1) * DEEP, :])
     for m in range(NM):
-        for k in range(KT):
-            pltpu.make_async_copy(leg.at[m, :, k], legv.at[m, k], lsem.at[m]).start()
-        coef_copy(m).start()
-    for m in range(NM):
-        pltpu.make_async_copy(legv.at[m], legv.at[m], lsem.at[m]).wait()
-        coef_copy(m).wait()
-        total = jnp.zeros((2 * NBLK, 2 * NS), F32)
-        for k in range(KT // 2):
-            pair = [legv.at[m, 2 * k + i].reshape(2 * NBLK, 128)[...] for i in range(2)]
-            total += dot(jnp.concatenate(pair, axis=1), coefv[m, k * 256 : (k + 1) * 256, :])
-        rounded = total.astype(BF)
+        rounded = totals[m].astype(BF)
         for c in range(2):
-            resv.at[m, c].reshape(2 * NBLK, 128)[...] = rounded[:, c * 128 : (c + 1) * 128]
-            pltpu.make_async_copy(resv.at[m, c], out.at[:, c, m], osem).start()
-    pltpu.make_async_copy(resv, resv, osem).wait()
+            out[:, c, m] = rounded[:, c * 128 : (c + 1) * 128].reshape(NBLK, 2, 128)
 
 
 def legendre_sums(legendre, coefficients):
@@ -92,16 +98,14 @@
         legendre_kernel,
         out_shape=jax.ShapeDtypeStruct((NBLK, 2, NM, 2, 128), BF),
         in_specs=[anywhere(), anywhere()],
-        out_specs=anywhere(),
+        out_specs=vmem(),
         scratch_shapes=[
-            pltpu.VMEM((NM, KT, NBLK, 2, 128), BF),
+            pltpu.VMEM((KT, NM, NBLK, 2, 128), BF),
             pltpu.VMEM((NM, L, 2 * NS), BF),
-            pltpu.VMEM((NM, 2, NBLK, 2, 128), BF),
-            pltpu.SemaphoreType.DMA((NM,)),
-            pltpu.SemaphoreType.DMA((NM,)),
-            pltpu.SemaphoreType.DMA,
+            pltpu.SemaphoreType.DMA((STEPS,)),
+            pltpu.SemaphoreType.DMA((STEPS,)),
         ],
-        compiler_params=params(60),
+        compiler_params=params(62),
         cost_estimate=pl.CostEstimate(flops=2 * NM * 128 * L * 256, bytes_accessed=6 * MB, transcendentals=0),
         name="legendre_sums",
     )(view, coefficients)
@@ -277,7 +281,7 @@
     xt[...] = holes.T
     groups = grp[...]
     lanes = lan[...]
-    base = obsm[...]
+    base = obsm[...].astype(F32)
 
     def copy(i):
         at = pl.ds(i * CHUNK * NG, CHUNK * NG)
@@ -286,10 +290,10 @@
     for i in range(NS // CHUNK):
         parts = [groups * xt[i * CHUNK + j : i * CHUNK + j + 1, :].astype(BF) for j in range(CHUNK)]
         got = dot(jnp.concatenate(parts, axis=0), lanes)
-        got = got.reshape(CHUNK * NG, 128).astype(BF)
+        got = got.reshape(CHUNK * NG, 128)
         for j in range(CHUNK):
             at = i * CHUNK * NG + j * NG
-            outv[at : at + NG, :] = got[j * NG : (j + 1) * NG, :] + base
+            outv[at : at + NG, :] = (got[j * NG : (j + 1) * NG, :] + base).astype(BF)
         copy(i).start()
     pltpu.make_async_copy(outv, outv, sem).wait()
 

time: 40.5 us -> 40 us (0.988)
  no operation moved by 1% of the time
where the time goes in v3:
time: 40 us; the launch traced here: 39.9 us
  starting transfers between devices  23.1 us (58%)
  Pallas kernels  11.8 us (30%)
  waiting for transfers between devices  4.86 us (12%)
    all_to_all x1, starting transfers between devices, body(): lax.all_to_all(sums, 'blk', split_axis=0, concat_axis=0, tiled=True)  13 us
    ppermute x6, starting transfers between devices, shifted(): return lax.ppermute(x, 'reg', [(i, (i + d) % NREG) for i in range(NREG)])  10.1 us
    pallas_call x1, Pallas kernels, legendre_sums(): pl.pallas_call(legendre_kernel, out_shape=jax.ShapeDtypeStruct((NBLK, 2,...  4.32 us
    all_to_all x1, waiting for transfers between devices, body(): lax.all_to_all(sums, 'blk', split_axis=0, concat_axis=0, tiled=True)  4.2 us
    pallas_call x1, Pallas kernels, prepare(): pl.pallas_call(prepare_kernel, out_shape=[jax.ShapeDtypeStruct(s, t) for...  3.86 us
    pallas_call x1, Pallas kernels, fill(): pl.pallas_call(fill_kernel, out_shape=jax.ShapeDtypeStruct((NS * NG, 128)...  2.31 us
    pallas_call x1, Pallas kernels, hole_sky(): pl.pallas_call(hole_kernel, out_shape=[jax.ShapeDtypeStruct((HMAX, NS), B...  1 us
  transfers between devices with their start and end apart: 7, of which 2 were waited for; matrix products, arithmetic and copies ran while one was open for 0% of the time, Pallas kernels for 13%

profile of v3, /device:TPU:1, one launch (start us, length us, event | category | flops | bytes accessed | tf_op | source)
XLA Modules:
  0.0 39.9 jit_solution(16978984200131361267)
XLA Ops:
  0.0 0.0 copy-start
  0.0 0.0 copy-start.2
  0.0 0.0 copy-start.3
  0.0 0.0 copy-start.4
  0.0 0.0 copy-start.5
  0.0 0.0 copy-start.1
  0.0 4.3 %legendre_sums.1 = bf16[64,2,4,2,128]{4,3,2,1,0:T(2,128)(2,1)} custom-call(bf16[4,64,16,2,128]{4,3,2,1,0:T(2,128)(2,1)} %bitcast.29, bf16[4,2048,256]{2,1,0:T(8,128)(2,1)} %coef.1), custom_call_target="tpu_custom_call" | custom-call | flops 536870912 | bytes 6291456 | tf_op jit(solution)/shard_map/legendre_sums/pallas_call | solution.py:97
  4.4 13.0 %all-to-all-start = ((bf16[64,2,4,2,128]{4,3,2,1,0:T(2,128)(2,1)}), bf16[64,2,4,2,128]{4,3,2,1,0:T(2,128)(2,1)S(1)}, u32[]{:S(2)}, u32[]{:S(2)}) async-start(bf16[64,2,4,2,128]{4,3,2,1,0:T(2,128)(2,1)} %legendre_sums.1), calls=%async_computation | async-start | bytes 524288 | tf_op jit(solution)/shard_map/all_to_all | solution.py:330
  17.4 0.0 copy-done
  17.4 1.4 %collective-permute-start.3 = (bf16[512,256]{1,0:T(8,128)(2,1)S(1)}, bf16[512,256]{1,0:T(8,128)(2,1)S(1)}, u32[]{:S(2)}, u32[]{:S(2)}) collective-permute-start(bf16[512,256]{1,0:T(8,128)(2,1)S(1)} %bitcast.21), channel_id=1, source_target_pairs={{0,1},{1,2},{2,3},{3,0},{4,5},{5,6},{6,7},{7,4},{8,9},{9,10},{10,1... | collective-permute-start | bytes 786440 | tf_op jit(solution)/shard_map/ppermute | solution.py:324
  18.8 2.6 %collective-permute-start.4 = (bf16[512,256]{1,0:T(8,128)(2,1)S(1)}, bf16[512,256]{1,0:T(8,128)(2,1)S(1)}, u32[]{:S(2)}, u32[]{:S(2)}) collective-permute-start(bf16[512,256]{1,0:T(8,128)(2,1)S(1)} %bitcast.22), channel_id=1, source_target_pairs={{0,2},{1,3},{2,0},{3,1},{4,6},{5,7},{6,4},{7,5},{8,10},{9,11},{10,... | collective-permute-start | bytes 786440 | tf_op jit(solution)/shard_map/ppermute | solution.py:324
  21.4 1.1 %collective-permute-start.5 = (bf16[512,256]{1,0:T(8,128)(2,1)S(1)}, bf16[512,256]{1,0:T(8,128)(2,1)S(1)}, u32[]{:S(2)}, u32[]{:S(2)}) collective-permute-start(bf16[512,256]{1,0:T(8,128)(2,1)S(1)} %bitcast.23), channel_id=1, source_target_pairs={{0,3},{1,0},{2,1},{3,2},{4,7},{5,4},{6,5},{7,6},{8,11},{9,8},{10,9... | collective-permute-start | bytes 786440 | tf_op jit(solution)/shard_map/ppermute | solution.py:324
  22.4 0.0 copy-done.2
  22.5 0.0 copy-done.3
  22.5 0.0 copy-done.4
  22.5 0.0 copy-done.5
  22.5 3.9 %prepare.1 = (bf16[256,1024]{1,0:T(8,128)(2,1)S(1)}, bf16[512,1024]{1,0:T(8,128)(2,1)S(1)}, f32[256,128]{1,0:T(8,128)S(1)}, bf16[32,512]{1,0:T(8,128)(2,1)S(1)},...) custom-call(s32[1]{0:T(128)} %bitcast.reg, s32[32,2,128]{2,1,0:T(2,128)S(1)} %bitcast.25, ...), custom_call_target="tpu_custom_call" | custom-call | flops 20000000 | bytes 8388608 | tf_op jit(solution)/shard_map/prepare/pallas_call | solution.py:210
  26.3 4.2 %all-to-all-done = bf16[64,2,4,2,128]{4,3,2,1,0:T(2,128)(2,1)S(1)} async-done(((bf16[64,2,4,2,128]{4,3,2,1,0:T(2,128)(2,1)}), bf16[64,2,4,2,128]{4,3,2,1,0:T(2,128)(2,1)S(1)}, u32[]{:S(2)}, u32[]{:S(2)}) %all-to-all-start) | async-done | bytes 262176 | tf_op jit(solution)/shard_map/all_to_all | solution.py:330
  30.5 0.3 residuals.1
  30.8 1.4 %collective-permute-start = (bf16[64,128]{1,0:T(8,128)(2,1)S(1)}, bf16[64,128]{1,0:T(8,128)(2,1)S(1)}, u32[]{:S(2)}, u32[]{:S(2)}) collective-permute-start(bf16[64,128]{1,0:T(8,128)(2,1)S(1)} %get-tuple-element.20), channel_id=1, source_target_pairs={{0,1},{1,2},{2,3},{3,0},{4,5},{5,6},{6,7},{7,4},{8,9},{9,10},{10,1... | collective-permute-start | bytes 49160 | tf_op jit(solution)/shard_map/ppermute | solution.py:324
  32.2 2.6 %collective-permute-start.1 = (bf16[64,128]{1,0:T(8,128)(2,1)S(1)}, bf16[64,128]{1,0:T(8,128)(2,1)S(1)}, u32[]{:S(2)}, u32[]{:S(2)}) collective-permute-start(bf16[64,128]{1,0:T(8,128)(2,1)S(1)} %get-tuple-element.21), channel_id=1, source_target_pairs={{0,2},{1,3},{2,0},{3,1},{4,6},{5,7},{6,4},{7,5},{8,10},{9,11},{10,... | collective-permute-start | bytes 49160 | tf_op jit(solution)/shard_map/ppermute | solution.py:324
  34.8 0.0 collective-permute-done.3.tile1
  34.8 1.1 %collective-permute-start.2 = (bf16[64,128]{1,0:T(8,128)(2,1)S(1)}, bf16[64,128]{1,0:T(8,128)(2,1)S(1)}, u32[]{:S(2)}, u32[]{:S(2)}) collective-permute-start(bf16[64,128]{1,0:T(8,128)(2,1)S(1)} %get-tuple-element.22), channel_id=1, source_target_pairs={{0,3},{1,0},{2,1},{3,2},{4,7},{5,4},{6,5},{7,6},{8,11},{9,8},{10,9... | collective-permute-start | bytes 49160 | tf_op jit(solution)/shard_map/ppermute | solution.py:324
  35.9 0.0 collective-permute-done.4.tile2
  35.9 0.0 collective-permute-done.5.tile3
  35.9 0.0 copy-done.1
  35.9 1.0 %hole_sky.1 = (bf16[512,128]{1,0:T(8,128)(2,1)S(1)}, bf16[512,256]{1,0:T(8,128)(2,1)S(1)}) custom-call(s32[1]{0:T(128)} %bitcast.reg, s32[1,4]{1,0:T(1,128)S(1)} %copy-done.1, bf16[1024,128]{1,0:T(8,128)(2,1)S(1)} %bitcast.20, bf16[512,1024]{1,0:T(8,128)(2,1)S(1)} %get-tuple-element.23.ph, bf16[512,256]{1,0:T(8,128)(2,1)S(1)} %bitcast.24, ...), custom_call_target="tpu_custom_call" | custom-call | flops 134217728 | bytes 2097152 | tf_op jit(solution)/shard_map/hole_sky/pallas_call | solution.py:260
  36.9 0.0 collective-permute-done.from1
  36.9 0.0 collective-permute-done.1.from2
  36.9 0.6 %collective-permute-done.2.from3 = bf16[64,128]{1,0:T(8,128)(2,1)S(1)} collective-permute-done((bf16[64,128]{1,0:T(8,128)(2,1)S(1)}, bf16[64,128]{1,0:T(8,128)(2,1)S(1)}, u32[]{:S(2)}, u32[]{:S(2)}) %collective-permute-start.2) | collective-permute-done | bytes 16416 | tf_op jit(solution)/shard_map/ppermute | solution.py:324
  37.6 2.3 %fill.1 = bf16[8192,128]{1,0:T(8,128)(2,1)} custom-call(s32[1]{0:T(128)} %bitcast.reg, bf16[64,128]{1,0:T(8,128)(2,1)S(1)} %get-tuple-element.19.after.own, bf16[64,128]{1,0:T(8,128)(2,1)S(1)} %collective-permute-done.from1, bf16[64,128]{1,0:T(8,128)(2,1)S(1)} %collective-permute-done.1.from2, bf16[64,128]{1,0:T(8,128)(2,1)S(1)} %collective-permute-done.2.from3, ...), custom_call_target="tpu_custom_call" | custom-call | flops 1073741824 | bytes 3145728 | tf_op jit(solution)/shard_map/fill/pallas_call | solution.py:302
Async XLA Ops:
  0.0 17.4 %copy-start = (bf16[1,1,512,256]{3,2,1,0:T(8,128)(2,1)S(1)}, bf16[1,1,512,256]{3,2,1,0:T(8,128)(2,1)}, u32[]{:S(2)}) copy-start(bf16[1,1,512,256]{3,2,1,0:T(8,128)(2,1)} %param.15) | copy-start | bytes 786436
  0.0 22.4 %copy-start.2 = (s32[2,4096]{1,0:T(2,128)S(1)}, s32[2,4096]{1,0:T(2,128)}, u32[]{:S(2)}) copy-start(s32[2,4096]{1,0:T(2,128)} %param.12) | copy-start | bytes 98308
  0.0 22.4 %copy-start.3 = (f32[2,4096]{1,0:T(2,128)S(1)}, f32[2,4096]{1,0:T(2,128)}, u32[]{:S(2)}) copy-start(f32[2,4096]{1,0:T(2,128)} %param.11) | copy-start | bytes 98308
  0.0 22.4 %copy-start.4 = (s32[1,4,256]{2,1,0:T(4,128)S(1)}, s32[1,4,256]{2,1,0:T(4,128)}, u32[]{:S(2)}) copy-start(s32[1,4,256]{2,1,0:T(4,128)} %param.13) | copy-start | bytes 12292
  0.0 22.4 %copy-start.5 = (s32[256]{0:T(256)S(1)}, s32[256]{0:T(256)}, u32[]{:S(2)}) copy-start(s32[256]{0:T(256)} %param.10) | copy-start | bytes 3076
  0.0 35.9 %copy-start.1 = (s32[1,4]{1,0:T(1,128)S(1)}, s32[1,4]{1,0:T(1,128)}, u32[]{:S(2)}) copy-start(s32[1,4]{1,0:T(1,128)} %owners.1) | copy-start | bytes 52
  4.4 26.2 %all-to-all-start = ((bf16[64,2,4,2,128]{4,3,2,1,0:T(2,128)(2,1)}), bf16[64,2,4,2,128]{4,3,2,1,0:T(2,128)(2,1)S(1)}, u32[]{:S(2)}, u32[]{:S(2)}) async-start(bf16[64,2,4,2,128]{4,3,2,1,0:T(2,128)(2,1)} %legendre_sums.1), calls=%async_computation | async-start | bytes 524288 | tf_op jit(solution)/shard_map/all_to_all | solution.py:330
  17.4 17.4 %collective-permute-start.3 = (bf16[512,256]{1,0:T(8,128)(2,1)S(1)}, bf16[512,256]{1,0:T(8,128)(2,1)S(1)}, u32[]{:S(2)}, u32[]{:S(2)}) collective-permute-start(bf16[512,256]{1,0:T(8,128)(2,1)S(1)} %bitcast.21), channel_id=1, source_target_pairs={{0,1},{1,2},{2,3},{3,0},{4,5},{5,6},{6,7},{7,4},{8,9},{9,10},{10,1... | collective-permute-start | bytes 786440 | tf_op jit(solution)/shard_map/ppermute | solution.py:324
  18.8 17.1 %collective-permute-start.4 = (bf16[512,256]{1,0:T(8,128)(2,1)S(1)}, bf16[512,256]{1,0:T(8,128)(2,1)S(1)}, u32[]{:S(2)}, u32[]{:S(2)}) collective-permute-start(bf16[512,256]{1,0:T(8,128)(2,1)S(1)} %bitcast.22), channel_id=1, source_target_pairs={{0,2},{1,3},{2,0},{3,1},{4,6},{5,7},{6,4},{7,5},{8,10},{9,11},{10,... | collective-permute-start | bytes 786440 | tf_op jit(solution)/shard_map/ppermute | solution.py:324
  21.4 14.5 %collective-permute-start.5 = (bf16[512,256]{1,0:T(8,128)(2,1)S(1)}, bf16[512,256]{1,0:T(8,128)(2,1)S(1)}, u32[]{:S(2)}, u32[]{:S(2)}) collective-permute-start(bf16[512,256]{1,0:T(8,128)(2,1)S(1)} %bitcast.23), channel_id=1, source_target_pairs={{0,3},{1,0},{2,1},{3,2},{4,7},{5,4},{6,5},{7,6},{8,11},{9,8},{10,9... | collective-permute-start | bytes 786440 | tf_op jit(solution)/shard_map/ppermute | solution.py:324
  30.8 6.1 %collective-permute-start = (bf16[64,128]{1,0:T(8,128)(2,1)S(1)}, bf16[64,128]{1,0:T(8,128)(2,1)S(1)}, u32[]{:S(2)}, u32[]{:S(2)}) collective-permute-start(bf16[64,128]{1,0:T(8,128)(2,1)S(1)} %get-tuple-element.20), channel_id=1, source_target_pairs={{0,1},{1,2},{2,3},{3,0},{4,5},{5,6},{6,7},{7,4},{8,9},{9,10},{10,1... | collective-permute-start | bytes 49160 | tf_op jit(solution)/shard_map/ppermute | solution.py:324
  32.2 4.7 %collective-permute-start.1 = (bf16[64,128]{1,0:T(8,128)(2,1)S(1)}, bf16[64,128]{1,0:T(8,128)(2,1)S(1)}, u32[]{:S(2)}, u32[]{:S(2)}) collective-permute-start(bf16[64,128]{1,0:T(8,128)(2,1)S(1)} %get-tuple-element.21), channel_id=1, source_target_pairs={{0,2},{1,3},{2,0},{3,1},{4,6},{5,7},{6,4},{7,5},{8,10},{9,11},{10,... | collective-permute-start | bytes 49160 | tf_op jit(solution)/shard_map/ppermute | solution.py:324
  34.8 2.8 %collective-permute-start.2 = (bf16[64,128]{1,0:T(8,128)(2,1)S(1)}, bf16[64,128]{1,0:T(8,128)(2,1)S(1)}, u32[]{:S(2)}, u32[]{:S(2)}) collective-permute-start(bf16[64,128]{1,0:T(8,128)(2,1)S(1)} %get-tuple-element.22), channel_id=1, source_target_pairs={{0,3},{1,0},{2,1},{3,2},{4,7},{5,4},{6,5},{7,6},{8,11},{9,8},{10,9... | collective-permute-start | bytes 49160 | tf_op jit(solution)/shard_map/ppermute | solution.py:324

commit v4 on v3

--- a/solution.py
+++ b/solution.py
@@ -246,20 +246,20 @@
 
 def hole_kernel(reg, owners, spectra, ph, tile0, tile1, tile2, tile3, after, sky, tile):
     del after
-    sky[...] = dot(ph[...], spectra[...]).astype(BF)
+    sky[...] = dot(ph[...], spectra[...]).T.astype(BF)
     me = reg[0]
     away = lax.rem(me - owners[0, me] + NREG, NREG)
     for d, ref in enumerate((tile0, tile1, tile2, tile3)):
 
         @pl.when(away == d)
         def _(ref=ref):
-            tile[...] = ref[...]
+            tile[...] = ref[...].T
 
 
 def hole_sky(reg, owners, spectra, ph, tiles, after):
     return pl.pallas_call(
         hole_kernel,
-        out_shape=[jax.ShapeDtypeStruct((HMAX, NS), BF), jax.ShapeDtypeStruct((HMAX, NB), BF)],
+        out_shape=[jax.ShapeDtypeStruct((NS, HMAX), BF), jax.ShapeDtypeStruct((NB, HMAX), BF)],
         in_specs=[smem(), smem()] + [vmem()] * 6 + [anywhere()],
         out_specs=[vmem()] * 2,
         compiler_params=params(30),
@@ -276,9 +276,8 @@
     for d, ref in enumerate((own, from1, from2, from3)):
         source = lax.rem(me - d + NREG, NREG)
         edge[pl.ds(pl.multiple_of(source * SLOTS, SLOTS), SLOTS), :] = ref[...]
-    correction = dot(tile[...], edge[...]).astype(BF)
-    holes = (sky[...].astype(F32) + correction.astype(F32)).astype(BF).astype(F32)
-    xt[...] = holes.T
+    correction = dot(edge[...].T, tile[...]).astype(BF)
+    xt[...] = (sky[...].astype(F32) + correction.astype(F32)).astype(BF).astype(F32)
     groups = grp[...]
     lanes = lan[...]
     base = obsm[...].astype(F32)

time: 40 us -> 40 us (level)
  no operation moved by 1% of the time
where the time goes in v4:
time: 40 us; the launch traced here: 39.8 us
  starting transfers between devices  23.1 us (58%)
  Pallas kernels  11.9 us (30%)
  waiting for transfers between devices  4.7 us (12%)
    all_to_all x1, starting transfers between devices, body(): lax.all_to_all(sums, 'blk', split_axis=0, concat_axis=0, tiled=True)  13 us
    ppermute x6, starting transfers between devices, shifted(): return lax.ppermute(x, 'reg', [(i, (i + d) % NREG) for i in range(NREG)])  10.1 us
    pallas_call x1, Pallas kernels, legendre_sums(): pl.pallas_call(legendre_kernel, out_shape=jax.ShapeDtypeStruct((NBLK, 2,...  4.32 us
    all_to_all x1, waiting for transfers between devices, body(): lax.all_to_all(sums, 'blk', split_axis=0, concat_axis=0, tiled=True)  4.2 us
    pallas_call x1, Pallas kernels, prepare(): pl.pallas_call(prepare_kernel, out_shape=[jax.ShapeDtypeStruct(s, t) for...  3.86 us
    pallas_call x1, Pallas kernels, fill(): pl.pallas_call(fill_kernel, out_shape=jax.ShapeDtypeStruct((NS * NG, 128)...  2.23 us
    pallas_call x1, Pallas kernels, hole_sky(): pl.pallas_call(hole_kernel, out_shape=[jax.ShapeDtypeStruct((NS, HMAX), B...  1.17 us
  transfers between devices with their start and end apart: 7, of which 2 were waited for; matrix products, arithmetic and copies ran while one was open for 0% of the time, Pallas kernels for 13%

profile of v4, /device:TPU:1, one launch (start us, length us, event | category | flops | bytes accessed | tf_op | source)
XLA Modules:
  0.0 39.8 jit_solution(16676853444239110114)
XLA Ops:
  0.0 0.0 copy-start
  0.0 0.0 copy-start.2
  0.0 0.0 copy-start.3
  0.0 0.0 copy-start.4
  0.0 0.0 copy-start.5
  0.0 0.0 copy-start.1
  0.0 4.3 %legendre_sums.1 = bf16[64,2,4,2,128]{4,3,2,1,0:T(2,128)(2,1)} custom-call(bf16[4,64,16,2,128]{4,3,2,1,0:T(2,128)(2,1)} %bitcast.29, bf16[4,2048,256]{2,1,0:T(8,128)(2,1)} %coef.1), custom_call_target="tpu_custom_call" | custom-call | flops 536870912 | bytes 6291456 | tf_op jit(solution)/shard_map/legendre_sums/pallas_call | solution.py:97
  4.4 13.0 %all-to-all-start = ((bf16[64,2,4,2,128]{4,3,2,1,0:T(2,128)(2,1)}), bf16[64,2,4,2,128]{4,3,2,1,0:T(2,128)(2,1)S(1)}, u32[]{:S(2)}, u32[]{:S(2)}) async-start(bf16[64,2,4,2,128]{4,3,2,1,0:T(2,128)(2,1)} %legendre_sums.1), calls=%async_computation | async-start | bytes 524288 | tf_op jit(solution)/shard_map/all_to_all | solution.py:329
  17.4 0.0 copy-done
  17.4 1.4 %collective-permute-start.3 = (bf16[512,256]{1,0:T(8,128)(2,1)S(1)}, bf16[512,256]{1,0:T(8,128)(2,1)S(1)}, u32[]{:S(2)}, u32[]{:S(2)}) collective-permute-start(bf16[512,256]{1,0:T(8,128)(2,1)S(1)} %bitcast.21), channel_id=1, source_target_pairs={{0,1},{1,2},{2,3},{3,0},{4,5},{5,6},{6,7},{7,4},{8,9},{9,10},{10,1... | collective-permute-start | bytes 786440 | tf_op jit(solution)/shard_map/ppermute | solution.py:323
  18.8 2.6 %collective-permute-start.4 = (bf16[512,256]{1,0:T(8,128)(2,1)S(1)}, bf16[512,256]{1,0:T(8,128)(2,1)S(1)}, u32[]{:S(2)}, u32[]{:S(2)}) collective-permute-start(bf16[512,256]{1,0:T(8,128)(2,1)S(1)} %bitcast.22), channel_id=1, source_target_pairs={{0,2},{1,3},{2,0},{3,1},{4,6},{5,7},{6,4},{7,5},{8,10},{9,11},{10,... | collective-permute-start | bytes 786440 | tf_op jit(solution)/shard_map/ppermute | solution.py:323
  21.4 1.1 %collective-permute-start.5 = (bf16[512,256]{1,0:T(8,128)(2,1)S(1)}, bf16[512,256]{1,0:T(8,128)(2,1)S(1)}, u32[]{:S(2)}, u32[]{:S(2)}) collective-permute-start(bf16[512,256]{1,0:T(8,128)(2,1)S(1)} %bitcast.23), channel_id=1, source_target_pairs={{0,3},{1,0},{2,1},{3,2},{4,7},{5,4},{6,5},{7,6},{8,11},{9,8},{10,9... | collective-permute-start | bytes 786440 | tf_op jit(solution)/shard_map/ppermute | solution.py:323
  22.4 0.0 copy-done.2
  22.5 0.0 copy-done.3
  22.5 0.0 copy-done.4
  22.5 0.0 copy-done.5
  22.5 3.9 %prepare.1 = (bf16[256,1024]{1,0:T(8,128)(2,1)S(1)}, bf16[512,1024]{1,0:T(8,128)(2,1)S(1)}, f32[256,128]{1,0:T(8,128)S(1)}, bf16[32,512]{1,0:T(8,128)(2,1)S(1)},...) custom-call(s32[1]{0:T(128)} %bitcast.reg, s32[32,2,128]{2,1,0:T(2,128)S(1)} %bitcast.25, ...), custom_call_target="tpu_custom_call" | custom-call | flops 20000000 | bytes 8388608 | tf_op jit(solution)/shard_map/prepare/pallas_call | solution.py:210
  26.3 4.2 %all-to-all-done = bf16[64,2,4,2,128]{4,3,2,1,0:T(2,128)(2,1)S(1)} async-done(((bf16[64,2,4,2,128]{4,3,2,1,0:T(2,128)(2,1)}), bf16[64,2,4,2,128]{4,3,2,1,0:T(2,128)(2,1)S(1)}, u32[]{:S(2)}, u32[]{:S(2)}) %all-to-all-start) | async-done | bytes 262176 | tf_op jit(solution)/shard_map/all_to_all | solution.py:329
  30.5 0.3 residuals.1
  30.8 1.4 %collective-permute-start = (bf16[64,128]{1,0:T(8,128)(2,1)S(1)}, bf16[64,128]{1,0:T(8,128)(2,1)S(1)}, u32[]{:S(2)}, u32[]{:S(2)}) collective-permute-start(bf16[64,128]{1,0:T(8,128)(2,1)S(1)} %get-tuple-element.20), channel_id=1, source_target_pairs={{0,1},{1,2},{2,3},{3,0},{4,5},{5,6},{6,7},{7,4},{8,9},{9,10},{10,1... | collective-permute-start | bytes 49160 | tf_op jit(solution)/shard_map/ppermute | solution.py:323
  32.2 2.6 %collective-permute-start.1 = (bf16[64,128]{1,0:T(8,128)(2,1)S(1)}, bf16[64,128]{1,0:T(8,128)(2,1)S(1)}, u32[]{:S(2)}, u32[]{:S(2)}) collective-permute-start(bf16[64,128]{1,0:T(8,128)(2,1)S(1)} %get-tuple-element.21), channel_id=1, source_target_pairs={{0,2},{1,3},{2,0},{3,1},{4,6},{5,7},{6,4},{7,5},{8,10},{9,11},{10,... | collective-permute-start | bytes 49160 | tf_op jit(solution)/shard_map/ppermute | solution.py:323
  34.8 0.0 collective-permute-done.3.tile1
  34.8 1.1 %collective-permute-start.2 = (bf16[64,128]{1,0:T(8,128)(2,1)S(1)}, bf16[64,128]{1,0:T(8,128)(2,1)S(1)}, u32[]{:S(2)}, u32[]{:S(2)}) collective-permute-start(bf16[64,128]{1,0:T(8,128)(2,1)S(1)} %get-tuple-element.22), channel_id=1, source_target_pairs={{0,3},{1,0},{2,1},{3,2},{4,7},{5,4},{6,5},{7,6},{8,11},{9,8},{10,9... | collective-permute-start | bytes 49160 | tf_op jit(solution)/shard_map/ppermute | solution.py:323
  35.9 0.0 collective-permute-done.4.tile2
  35.9 0.0 collective-permute-done.5.tile3
  35.9 0.0 copy-done.1
  35.9 1.2 %hole_sky.1 = (bf16[128,512]{1,0:T(8,128)(2,1)S(1)}, bf16[256,512]{1,0:T(8,128)(2,1)S(1)}) custom-call(s32[1]{0:T(128)} %bitcast.reg, s32[1,4]{1,0:T(1,128)S(1)} %copy-done.1, bf16[1024,128]{1,0:T(8,128)(2,1)S(1)} %bitcast.20, bf16[512,1024]{1,0:T(8,128)(2,1)S(1)} %get-tuple-element.23.ph, bf16[512,256]{1,0:T(8,128)(2,1)S(1)} %bitcast.24, ...), custom_call_target="tpu_custom_call" | custom-call | flops 134217728 | bytes 2097152 | tf_op jit(solution)/shard_map/hole_sky/pallas_call | solution.py:260
  37.1 0.0 collective-permute-done.from1
  37.1 0.0 collective-permute-done.1.from2
  37.1 0.5 %collective-permute-done.2.from3 = bf16[64,128]{1,0:T(8,128)(2,1)S(1)} collective-permute-done((bf16[64,128]{1,0:T(8,128)(2,1)S(1)}, bf16[64,128]{1,0:T(8,128)(2,1)S(1)}, u32[]{:S(2)}, u32[]{:S(2)}) %collective-permute-start.2) | collective-permute-done | bytes 16416 | tf_op jit(solution)/shard_map/ppermute | solution.py:323
  37.6 2.2 %fill.1 = bf16[8192,128]{1,0:T(8,128)(2,1)} custom-call(s32[1]{0:T(128)} %bitcast.reg, bf16[64,128]{1,0:T(8,128)(2,1)S(1)} %get-tuple-element.19.after.own, bf16[64,128]{1,0:T(8,128)(2,1)S(1)} %collective-permute-done.from1, bf16[64,128]{1,0:T(8,128)(2,1)S(1)} %collective-permute-done.1.from2, bf16[64,128]{1,0:T(8,128)(2,1)S(1)} %collective-permute-done.2.from3, ...), custom_call_target="tpu_custom_call" | custom-call | flops 1073741824 | bytes 3145728 | tf_op jit(solution)/shard_map/fill/pallas_call | solution.py:301
Async XLA Ops:
  0.0 17.4 %copy-start = (bf16[1,1,512,256]{3,2,1,0:T(8,128)(2,1)S(1)}, bf16[1,1,512,256]{3,2,1,0:T(8,128)(2,1)}, u32[]{:S(2)}) copy-start(bf16[1,1,512,256]{3,2,1,0:T(8,128)(2,1)} %param.15) | copy-start | bytes 786436
  0.0 22.4 %copy-start.2 = (s32[2,4096]{1,0:T(2,128)S(1)}, s32[2,4096]{1,0:T(2,128)}, u32[]{:S(2)}) copy-start(s32[2,4096]{1,0:T(2,128)} %param.12) | copy-start | bytes 98308
  0.0 22.4 %copy-start.3 = (f32[2,4096]{1,0:T(2,128)S(1)}, f32[2,4096]{1,0:T(2,128)}, u32[]{:S(2)}) copy-start(f32[2,4096]{1,0:T(2,128)} %param.11) | copy-start | bytes 98308
  0.0 22.4 %copy-start.4 = (s32[1,4,256]{2,1,0:T(4,128)S(1)}, s32[1,4,256]{2,1,0:T(4,128)}, u32[]{:S(2)}) copy-start(s32[1,4,256]{2,1,0:T(4,128)} %param.13) | copy-start | bytes 12292
  0.0 22.4 %copy-start.5 = (s32[256]{0:T(256)S(1)}, s32[256]{0:T(256)}, u32[]{:S(2)}) copy-start(s32[256]{0:T(256)} %param.10) | copy-start | bytes 3076
  0.0 35.9 %copy-start.1 = (s32[1,4]{1,0:T(1,128)S(1)}, s32[1,4]{1,0:T(1,128)}, u32[]{:S(2)}) copy-start(s32[1,4]{1,0:T(1,128)} %owners.1) | copy-start | bytes 52
  4.4 26.2 %all-to-all-start = ((bf16[64,2,4,2,128]{4,3,2,1,0:T(2,128)(2,1)}), bf16[64,2,4,2,128]{4,3,2,1,0:T(2,128)(2,1)S(1)}, u32[]{:S(2)}, u32[]{:S(2)}) async-start(bf16[64,2,4,2,128]{4,3,2,1,0:T(2,128)(2,1)} %legendre_sums.1), calls=%async_computation | async-start | bytes 524288 | tf_op jit(solution)/shard_map/all_to_all | solution.py:329
  17.4 17.4 %collective-permute-start.3 = (bf16[512,256]{1,0:T(8,128)(2,1)S(1)}, bf16[512,256]{1,0:T(8,128)(2,1)S(1)}, u32[]{:S(2)}, u32[]{:S(2)}) collective-permute-start(bf16[512,256]{1,0:T(8,128)(2,1)S(1)} %bitcast.21), channel_id=1, source_target_pairs={{0,1},{1,2},{2,3},{3,0},{4,5},{5,6},{6,7},{7,4},{8,9},{9,10},{10,1... | collective-permute-start | bytes 786440 | tf_op jit(solution)/shard_map/ppermute | solution.py:323
  18.8 17.1 %collective-permute-start.4 = (bf16[512,256]{1,0:T(8,128)(2,1)S(1)}, bf16[512,256]{1,0:T(8,128)(2,1)S(1)}, u32[]{:S(2)}, u32[]{:S(2)}) collective-permute-start(bf16[512,256]{1,0:T(8,128)(2,1)S(1)} %bitcast.22), channel_id=1, source_target_pairs={{0,2},{1,3},{2,0},{3,1},{4,6},{5,7},{6,4},{7,5},{8,10},{9,11},{10,... | collective-permute-start | bytes 786440 | tf_op jit(solution)/shard_map/ppermute | solution.py:323
  21.4 14.5 %collective-permute-start.5 = (bf16[512,256]{1,0:T(8,128)(2,1)S(1)}, bf16[512,256]{1,0:T(8,128)(2,1)S(1)}, u32[]{:S(2)}, u32[]{:S(2)}) collective-permute-start(bf16[512,256]{1,0:T(8,128)(2,1)S(1)} %bitcast.23), channel_id=1, source_target_pairs={{0,3},{1,0},{2,1},{3,2},{4,7},{5,4},{6,5},{7,6},{8,11},{9,8},{10,9... | collective-permute-start | bytes 786440 | tf_op jit(solution)/shard_map/ppermute | solution.py:323
  30.8 6.3 %collective-permute-start = (bf16[64,128]{1,0:T(8,128)(2,1)S(1)}, bf16[64,128]{1,0:T(8,128)(2,1)S(1)}, u32[]{:S(2)}, u32[]{:S(2)}) collective-permute-start(bf16[64,128]{1,0:T(8,128)(2,1)S(1)} %get-tuple-element.20), channel_id=1, source_target_pairs={{0,1},{1,2},{2,3},{3,0},{4,5},{5,6},{6,7},{7,4},{8,9},{9,10},{10,1... | collective-permute-start | bytes 49160 | tf_op jit(solution)/shard_map/ppermute | solution.py:323
  32.2 4.9 %collective-permute-start.1 = (bf16[64,128]{1,0:T(8,128)(2,1)S(1)}, bf16[64,128]{1,0:T(8,128)(2,1)S(1)}, u32[]{:S(2)}, u32[]{:S(2)}) collective-permute-start(bf16[64,128]{1,0:T(8,128)(2,1)S(1)} %get-tuple-element.21), channel_id=1, source_target_pairs={{0,2},{1,3},{2,0},{3,1},{4,6},{5,7},{6,4},{7,5},{8,10},{9,11},{10,... | collective-permute-start | bytes 49160 | tf_op jit(solution)/shard_map/ppermute | solution.py:323
  34.8 2.8 %collective-permute-start.2 = (bf16[64,128]{1,0:T(8,128)(2,1)S(1)}, bf16[64,128]{1,0:T(8,128)(2,1)S(1)}, u32[]{:S(2)}, u32[]{:S(2)}) collective-permute-start(bf16[64,128]{1,0:T(8,128)(2,1)S(1)} %get-tuple-element.22), channel_id=1, source_target_pairs={{0,3},{1,0},{2,1},{3,2},{4,7},{5,4},{6,5},{7,6},{8,11},{9,8},{10,9... | collective-permute-start | bytes 49160 | tf_op jit(solution)/shard_map/ppermute | solution.py:323

commit v5 on v4

--- a/solution.py
+++ b/solution.py
@@ -225,28 +225,30 @@
     )(reg, holes, observed, boundary, orders)
 
 
-def residual_kernel(spectra, pb, obsb, own, to1, to2, to3):
-    sky = dot(pb[...], spectra[...]).astype(BF).astype(F32)
-    residual = (obsb[...] - sky).astype(BF)
-    for d, ref in enumerate((own, to1, to2, to3)):
+def residual_kernel(spectra, pb, obsb, *away):
+    sky = dot(pb[SLOTS:], spectra[...]).astype(BF).astype(F32)
+    residual = (obsb[SLOTS:] - sky).astype(BF)
+    for d, ref in enumerate(away):
         ref[...] = residual[d * SLOTS : (d + 1) * SLOTS, :]
 
 
 def residuals(spectra, pb, obsb):
     return pl.pallas_call(
         residual_kernel,
-        out_shape=[jax.ShapeDtypeStruct((SLOTS, NS), BF)] * NREG,
+        out_shape=[jax.ShapeDtypeStruct((SLOTS, NS), BF)] * (NREG - 1),
         in_specs=[vmem()] * 3,
-        out_specs=[vmem()] * NREG,
+        out_specs=[vmem()] * (NREG - 1),
         compiler_params=params(30),
-        cost_estimate=pl.CostEstimate(flops=2 * NB * NK * NS, bytes_accessed=MB, transcendentals=0),
+        cost_estimate=pl.CostEstimate(flops=2 * (NB - SLOTS) * NK * NS, bytes_accessed=MB, transcendentals=0),
         name="residuals",
     )(spectra, pb, obsb)
 
 
-def hole_kernel(reg, owners, spectra, ph, tile0, tile1, tile2, tile3, after, sky, tile):
+def hole_kernel(reg, owners, spectra, ph, pb, obsb, tile0, tile1, tile2, tile3, after, sky, tile, own):
     del after
     sky[...] = dot(ph[...], spectra[...]).T.astype(BF)
+    edge = dot(pb[0:SLOTS], spectra[...]).astype(BF).astype(F32)
+    own[...] = (obsb[0:SLOTS] - edge).astype(BF)
     me = reg[0]
     away = lax.rem(me - owners[0, me] + NREG, NREG)
     for d, ref in enumerate((tile0, tile1, tile2, tile3)):
@@ -256,16 +258,16 @@
             tile[...] = ref[...].T
 
 
-def hole_sky(reg, owners, spectra, ph, tiles, after):
+def hole_sky(reg, owners, spectra, ph, pb, obsb, tiles, after):
     return pl.pallas_call(
         hole_kernel,
-        out_shape=[jax.ShapeDtypeStruct((NS, HMAX), BF), jax.ShapeDtypeStruct((NB, HMAX), BF)],
-        in_specs=[smem(), smem()] + [vmem()] * 6 + [anywhere()],
-        out_specs=[vmem()] * 2,
+        out_shape=[jax.ShapeDtypeStruct(s, BF) for s in ((NS, HMAX), (NB, HMAX), (SLOTS, NS))],
+        in_specs=[smem(), smem()] + [vmem()] * 8 + [anywhere()],
+        out_specs=[vmem()] * 3,
         compiler_params=params(30),
         cost_estimate=pl.CostEstimate(flops=2 * HMAX * NK * NS, bytes_accessed=2 * MB, transcendentals=0),
         name="hole_sky",
-    )(reg, owners, spectra, ph, *tiles, after)
+    )(reg, owners, spectra, ph, pb, obsb, *tiles, after)
 
 
 CHUNK = 8
@@ -332,10 +334,10 @@
     )
     tile = kriging.reshape(HMAX, NB)
     tiles = [tile] + [shifted(tile, d) for d in (1, 2, 3)]
-    own, *away = residuals(spectra, pb, obsb)
-    edges = [own] + [shifted(x, d + 1) for d, x in enumerate(away)]
-    sky, my_tile = hole_sky(reg, tile_owner, spectra, ph, tiles, own)
-    out = fill(reg, edges, my_tile, sky, grp, lan, obsm)
+    away = residuals(spectra, pb, obsb)
+    edges = [shifted(x, d + 1) for d, x in enumerate(away)]
+    sky, my_tile, own = hole_sky(reg, tile_owner, spectra, ph, pb, obsb, tiles, away[2])
+    out = fill(reg, [own] + edges, my_tile, sky, grp, lan, obsm)
     return out.reshape(NS, NPHI // 128, 2, 128).transpose(0, 2, 1, 3).reshape(NS, 2, NPHI)
 
 

time: 40 us -> 39.9 us (level)
  starting transfers between devices: 23.1 us -> 21.9 us
  waiting for transfers between devices: 4.7 us -> 5.86 us
    ppermute x6, starting transfers between devices: 10.1 us -> 8.91 us  [shifted(): return lax.ppermute(x, 'reg', [(i, (i + d) % NREG) for i in range(NREG)])]
    all_to_all x1, waiting for transfers between devices: 4.2 us -> 5.41 us  [body(): lax.all_to_all(sums, 'blk', split_axis=0, concat_axis=0, tiled=True)]
where the time goes in v5:
time: 39.9 us; the launch traced here: 39.8 us
  starting transfers between devices  21.9 us (55%)
  Pallas kernels  11.9 us (30%)
  waiting for transfers between devices  5.86 us (15%)
    all_to_all x1, starting transfers between devices, body(): lax.all_to_all(sums, 'blk', split_axis=0, concat_axis=0, tiled=True)  13 us
    ppermute x6, starting transfers between devices, shifted(): return lax.ppermute(x, 'reg', [(i, (i + d) % NREG) for i in range(NREG)])  8.91 us
    all_to_all x1, waiting for transfers between devices, body(): lax.all_to_all(sums, 'blk', split_axis=0, concat_axis=0, tiled=True)  5.41 us
    pallas_call x1, Pallas kernels, legendre_sums(): pl.pallas_call(legendre_kernel, out_shape=jax.ShapeDtypeStruct((NBLK, 2,...  4.32 us
    pallas_call x1, Pallas kernels, prepare(): pl.pallas_call(prepare_kernel, out_shape=[jax.ShapeDtypeStruct(s, t) for...  3.87 us
    pallas_call x1, Pallas kernels, fill(): pl.pallas_call(fill_kernel, out_shape=jax.ShapeDtypeStruct((NS * NG, 128)...  2.22 us
    pallas_call x1, Pallas kernels, hole_sky(): pl.pallas_call(hole_kernel, out_shape=[jax.ShapeDtypeStruct(s, BF) for s...  1.21 us
  transfers between devices with their start and end apart: 7, of which 2 were waited for; matrix products, arithmetic and copies ran while one was open for 0% of the time, Pallas kernels for 13%

profile of v5, /device:TPU:1, one launch (start us, length us, event | category | flops | bytes accessed | tf_op | source)
XLA Modules:
  0.0 39.8 jit_solution(11647510260175598281)
XLA Ops:
  0.0 0.0 copy-start
  0.0 0.0 copy-start.2
  0.0 0.0 copy-start.3
  0.0 0.0 copy-start.4
  0.0 0.0 copy-start.5
  0.0 0.0 copy-start.1
  0.0 4.3 %legendre_sums.1 = bf16[64,2,4,2,128]{4,3,2,1,0:T(2,128)(2,1)} custom-call(bf16[4,64,16,2,128]{4,3,2,1,0:T(2,128)(2,1)} %bitcast.29, bf16[4,2048,256]{2,1,0:T(8,128)(2,1)} %coef.1), custom_call_target="tpu_custom_call" | custom-call | flops 536870912 | bytes 6291456 | tf_op jit(solution)/shard_map/legendre_sums/pallas_call | solution.py:97
  4.4 13.0 %all-to-all-start = ((bf16[64,2,4,2,128]{4,3,2,1,0:T(2,128)(2,1)}), bf16[64,2,4,2,128]{4,3,2,1,0:T(2,128)(2,1)S(1)}, u32[]{:S(2)}, u32[]{:S(2)}) async-start(bf16[64,2,4,2,128]{4,3,2,1,0:T(2,128)(2,1)} %legendre_sums.1), calls=%async_computation | async-start | bytes 524288 | tf_op jit(solution)/shard_map/all_to_all | solution.py:331
  17.4 0.0 copy-done
  17.4 2.8 %collective-permute-start.2 = (bf16[512,256]{1,0:T(8,128)(2,1)S(1)}, bf16[512,256]{1,0:T(8,128)(2,1)S(1)}, u32[]{:S(2)}, u32[]{:S(2)}) collective-permute-start(bf16[512,256]{1,0:T(8,128)(2,1)S(1)} %bitcast.21), channel_id=1, source_target_pairs={{0,3},{1,0},{2,1},{3,2},{4,7},{5,4},{6,5},{7,6},{8,11},{9,8},{10,9... | collective-permute-start | bytes 786440 | tf_op jit(solution)/shard_map/ppermute | solution.py:325
  20.2 0.3 collective-permute-start.1
  20.5 0.7 %collective-permute-start = (bf16[512,256]{1,0:T(8,128)(2,1)S(1)}, bf16[512,256]{1,0:T(8,128)(2,1)S(1)}, u32[]{:S(2)}, u32[]{:S(2)}) collective-permute-start(bf16[512,256]{1,0:T(8,128)(2,1)S(1)} %bitcast.23), channel_id=1, source_target_pairs={{0,1},{1,2},{2,3},{3,0},{4,5},{5,6},{6,7},{7,4},{8,9},{9,10},{10,1... | collective-permute-start | bytes 786440 | tf_op jit(solution)/shard_map/ppermute | solution.py:325
  21.2 0.0 copy-done.2
  21.2 0.0 copy-done.3
  21.2 0.0 copy-done.4
  21.2 0.0 copy-done.5
  21.3 3.9 %prepare.1 = (bf16[256,1024]{1,0:T(8,128)(2,1)S(1)}, bf16[512,1024]{1,0:T(8,128)(2,1)S(1)}, f32[256,128]{1,0:T(8,128)S(1)}, bf16[32,512]{1,0:T(8,128)(2,1)S(1)},...) custom-call(s32[1]{0:T(128)} %bitcast.reg, s32[32,2,128]{2,1,0:T(2,128)S(1)} %bitcast.25, ...), custom_call_target="tpu_custom_call" | custom-call | flops 20000000 | bytes 8388608 | tf_op jit(solution)/shard_map/prepare/pallas_call | solution.py:210
  25.1 5.4 %all-to-all-done = bf16[64,2,4,2,128]{4,3,2,1,0:T(2,128)(2,1)S(1)} async-done(((bf16[64,2,4,2,128]{4,3,2,1,0:T(2,128)(2,1)}), bf16[64,2,4,2,128]{4,3,2,1,0:T(2,128)(2,1)S(1)}, u32[]{:S(2)}, u32[]{:S(2)}) %all-to-all-start) | async-done | bytes 262176 | tf_op jit(solution)/shard_map/all_to_all | solution.py:331
  30.5 0.3 residuals.1
  30.8 1.4 %collective-permute-start.3 = (bf16[64,128]{1,0:T(8,128)(2,1)S(1)}, bf16[64,128]{1,0:T(8,128)(2,1)S(1)}, u32[]{:S(2)}, u32[]{:S(2)}) collective-permute-start(bf16[64,128]{1,0:T(8,128)(2,1)S(1)} %get-tuple-element.22), channel_id=1, source_target_pairs={{0,1},{1,2},{2,3},{3,0},{4,5},{5,6},{6,7},{7,4},{8,9},{9,10},{10,1... | collective-permute-start | bytes 49160 | tf_op jit(solution)/shard_map/ppermute | solution.py:325
  32.2 2.6 %collective-permute-start.4 = (bf16[64,128]{1,0:T(8,128)(2,1)S(1)}, bf16[64,128]{1,0:T(8,128)(2,1)S(1)}, u32[]{:S(2)}, u32[]{:S(2)}) collective-permute-start(bf16[64,128]{1,0:T(8,128)(2,1)S(1)} %get-tuple-element.23), channel_id=1, source_target_pairs={{0,2},{1,3},{2,0},{3,1},{4,6},{5,7},{6,4},{7,5},{8,10},{9,11},{10,... | collective-permute-start | bytes 49160 | tf_op jit(solution)/shard_map/ppermute | solution.py:325
  34.8 0.0 collective-permute-done.2.tile3
  34.8 1.1 %collective-permute-start.5 = (bf16[64,128]{1,0:T(8,128)(2,1)S(1)}, bf16[64,128]{1,0:T(8,128)(2,1)S(1)}, u32[]{:S(2)}, u32[]{:S(2)}) collective-permute-start(bf16[64,128]{1,0:T(8,128)(2,1)S(1)} %get-tuple-element.20.after), channel_id=1, source_target_pairs={{0,3},{1,0},{2,1},{3,2},{4,7},{5,4},{6,5},{7,6},{8,11},{9,8},{10,9... | collective-permute-start | bytes 49160 | tf_op jit(solution)/shard_map/ppermute | solution.py:325
  35.9 0.0 collective-permute-done.1.tile2
  35.9 0.0 collective-permute-done.tile1
  35.9 0.0 copy-done.1
  35.9 1.2 %hole_sky.1 = (bf16[128,512]{1,0:T(8,128)(2,1)S(1)}, bf16[256,512]{1,0:T(8,128)(2,1)S(1)}, bf16[64,128]{1,0:T(8,128)(2,1)S(1)}) custom-call(s32[1]{0:T(128)} %bitcast.reg, s32[1,4]{1,0:T(1,128)S(1)} %copy-done.1, bf16[1024,128]{1,0:T(8,128)(2,1)S(1)} %bitcast.20, bf16[512,1024]{1,0:T(8,128)(2,1)S(1)} %get-tuple-element.17.ph, ...), custom_call_target="tpu_custom_call" | custom-call | flops 134217728 | bytes 2097152 | tf_op jit(solution)/shard_map/hole_sky/pallas_call | solution.py:262
  37.1 0.0 collective-permute-done.3.from1
  37.1 0.0 collective-permute-done.4.from2
  37.1 0.4 %collective-permute-done.5.from3 = bf16[64,128]{1,0:T(8,128)(2,1)S(1)} collective-permute-done((bf16[64,128]{1,0:T(8,128)(2,1)S(1)}, bf16[64,128]{1,0:T(8,128)(2,1)S(1)}, u32[]{:S(2)}, u32[]{:S(2)}) %collective-permute-start.5) | collective-permute-done | bytes 16416 | tf_op jit(solution)/shard_map/ppermute | solution.py:325
  37.6 2.2 %fill.1 = bf16[8192,128]{1,0:T(8,128)(2,1)} custom-call(s32[1]{0:T(128)} %bitcast.reg, bf16[64,128]{1,0:T(8,128)(2,1)S(1)} %get-tuple-element.21.own, bf16[64,128]{1,0:T(8,128)(2,1)S(1)} %collective-permute-done.3.from1, bf16[64,128]{1,0:T(8,128)(2,1)S(1)} %collective-permute-done.4.from2, bf16[64,128]{1,0:T(8,128)(2,1)S(1)} %collective-permute-done.5.from3, ...), custom_call_target="tpu_custom_call" | custom-call | flops 1073741824 | bytes 3145728 | tf_op jit(solution)/shard_map/fill/pallas_call | solution.py:303
Async XLA Ops:
  0.0 17.4 %copy-start = (bf16[1,1,512,256]{3,2,1,0:T(8,128)(2,1)S(1)}, bf16[1,1,512,256]{3,2,1,0:T(8,128)(2,1)}, u32[]{:S(2)}) copy-start(bf16[1,1,512,256]{3,2,1,0:T(8,128)(2,1)} %param.15) | copy-start | bytes 786436
  0.0 21.2 %copy-start.2 = (s32[2,4096]{1,0:T(2,128)S(1)}, s32[2,4096]{1,0:T(2,128)}, u32[]{:S(2)}) copy-start(s32[2,4096]{1,0:T(2,128)} %param.12) | copy-start | bytes 98308
  0.0 21.2 %copy-start.3 = (f32[2,4096]{1,0:T(2,128)S(1)}, f32[2,4096]{1,0:T(2,128)}, u32[]{:S(2)}) copy-start(f32[2,4096]{1,0:T(2,128)} %param.11) | copy-start | bytes 98308
  0.0 21.2 %copy-start.4 = (s32[1,4,256]{2,1,0:T(4,128)S(1)}, s32[1,4,256]{2,1,0:T(4,128)}, u32[]{:S(2)}) copy-start(s32[1,4,256]{2,1,0:T(4,128)} %param.13) | copy-start | bytes 12292
  0.0 21.2 %copy-start.5 = (s32[256]{0:T(256)S(1)}, s32[256]{0:T(256)}, u32[]{:S(2)}) copy-start(s32[256]{0:T(256)} %param.10) | copy-start | bytes 3076
  0.0 35.8 %copy-start.1 = (s32[1,4]{1,0:T(1,128)S(1)}, s32[1,4]{1,0:T(1,128)}, u32[]{:S(2)}) copy-start(s32[1,4]{1,0:T(1,128)} %owners.1) | copy-start | bytes 52
  4.4 26.2 %all-to-all-start = ((bf16[64,2,4,2,128]{4,3,2,1,0:T(2,128)(2,1)}), bf16[64,2,4,2,128]{4,3,2,1,0:T(2,128)(2,1)S(1)}, u32[]{:S(2)}, u32[]{:S(2)}) async-start(bf16[64,2,4,2,128]{4,3,2,1,0:T(2,128)(2,1)} %legendre_sums.1), calls=%async_computation | async-start | bytes 524288 | tf_op jit(solution)/shard_map/all_to_all | solution.py:331
  17.4 17.4 %collective-permute-start.2 = (bf16[512,256]{1,0:T(8,128)(2,1)S(1)}, bf16[512,256]{1,0:T(8,128)(2,1)S(1)}, u32[]{:S(2)}, u32[]{:S(2)}) collective-permute-start(bf16[512,256]{1,0:T(8,128)(2,1)S(1)} %bitcast.21), channel_id=1, source_target_pairs={{0,3},{1,0},{2,1},{3,2},{4,7},{5,4},{6,5},{7,6},{8,11},{9,8},{10,9... | collective-permute-start | bytes 786440 | tf_op jit(solution)/shard_map/ppermute | solution.py:325
  20.2 15.7 %collective-permute-start.1 = (bf16[512,256]{1,0:T(8,128)(2,1)S(1)}, bf16[512,256]{1,0:T(8,128)(2,1)S(1)}, u32[]{:S(2)}, u32[]{:S(2)}) collective-permute-start(bf16[512,256]{1,0:T(8,128)(2,1)S(1)} %bitcast.22), channel_id=1, source_target_pairs={{0,2},{1,3},{2,0},{3,1},{4,6},{5,7},{6,4},{7,5},{8,10},{9,11},{10,... | collective-permute-start | bytes 786440 | tf_op jit(solution)/shard_map/ppermute | solution.py:325
  20.5 15.3 %collective-permute-start = (bf16[512,256]{1,0:T(8,128)(2,1)S(1)}, bf16[512,256]{1,0:T(8,128)(2,1)S(1)}, u32[]{:S(2)}, u32[]{:S(2)}) collective-permute-start(bf16[512,256]{1,0:T(8,128)(2,1)S(1)} %bitcast.23), channel_id=1, source_target_pairs={{0,1},{1,2},{2,3},{3,0},{4,5},{5,6},{6,7},{7,4},{8,9},{9,10},{10,1... | collective-permute-start | bytes 786440 | tf_op jit(solution)/shard_map/ppermute | solution.py:325
  30.8 6.3 %collective-permute-start.3 = (bf16[64,128]{1,0:T(8,128)(2,1)S(1)}, bf16[64,128]{1,0:T(8,128)(2,1)S(1)}, u32[]{:S(2)}, u32[]{:S(2)}) collective-permute-start(bf16[64,128]{1,0:T(8,128)(2,1)S(1)} %get-tuple-element.22), channel_id=1, source_target_pairs={{0,1},{1,2},{2,3},{3,0},{4,5},{5,6},{6,7},{7,4},{8,9},{9,10},{10,1... | collective-permute-start | bytes 49160 | tf_op jit(solution)/shard_map/ppermute | solution.py:325
  32.2 4.9 %collective-permute-start.4 = (bf16[64,128]{1,0:T(8,128)(2,1)S(1)}, bf16[64,128]{1,0:T(8,128)(2,1)S(1)}, u32[]{:S(2)}, u32[]{:S(2)}) collective-permute-start(bf16[64,128]{1,0:T(8,128)(2,1)S(1)} %get-tuple-element.23), channel_id=1, source_target_pairs={{0,2},{1,3},{2,0},{3,1},{4,6},{5,7},{6,4},{7,5},{8,10},{9,11},{10,... | collective-permute-start | bytes 49160 | tf_op jit(solution)/shard_map/ppermute | solution.py:325
  34.8 2.8 %collective-permute-start.5 = (bf16[64,128]{1,0:T(8,128)(2,1)S(1)}, bf16[64,128]{1,0:T(8,128)(2,1)S(1)}, u32[]{:S(2)}, u32[]{:S(2)}) collective-permute-start(bf16[64,128]{1,0:T(8,128)(2,1)S(1)} %get-tuple-element.20.after), channel_id=1, source_target_pairs={{0,3},{1,0},{2,1},{3,2},{4,7},{5,4},{6,5},{7,6},{8,11},{9,8},{10,9... | collective-permute-start | bytes 49160 | tf_op jit(solution)/shard_map/ppermute | solution.py:325

commit v6 on v4

--- a/solution.py
+++ b/solution.py
@@ -287,8 +287,9 @@
         return pltpu.make_async_copy(outv.at[at], out.at[at], sem)
 
     for i in range(NS // CHUNK):
-        parts = [groups * xt[i * CHUNK + j : i * CHUNK + j + 1, :].astype(BF) for j in range(CHUNK)]
-        got = dot(jnp.concatenate(parts, axis=0), lanes)
+        lines = xt[i * CHUNK : (i + 1) * CHUNK, :].astype(BF)
+        left = lines[:, None, :] * groups[None]
+        got = dot(left.reshape(CHUNK * NT, HMAX), lanes)
         got = got.reshape(CHUNK * NG, 128)
         for j in range(CHUNK):
             at = i * CHUNK * NG + j * NG

time: 40 us -> 39.9 us (level)
  no operation moved by 1% of the time
where the time goes in v6:
time: 39.9 us; the launch traced here: 39.8 us
  starting transfers between devices  23.1 us (58%)
  Pallas kernels  11.8 us (30%)
  waiting for transfers between devices  4.69 us (12%)
    all_to_all x1, starting transfers between devices, body(): lax.all_to_all(sums, 'blk', split_axis=0, concat_axis=0, tiled=True)  13 us
    ppermute x6, starting transfers between devices, shifted(): return lax.ppermute(x, 'reg', [(i, (i + d) % NREG) for i in range(NREG)])  10.1 us
    pallas_call x1, Pallas kernels, legendre_sums(): pl.pallas_call(legendre_kernel, out_shape=jax.ShapeDtypeStruct((NBLK, 2,...  4.32 us
    all_to_all x1, waiting for transfers between devices, body(): lax.all_to_all(sums, 'blk', split_axis=0, concat_axis=0, tiled=True)  4.2 us
    pallas_call x1, Pallas kernels, prepare(): pl.pallas_call(prepare_kernel, out_shape=[jax.ShapeDtypeStruct(s, t) for...  3.86 us
    pallas_call x1, Pallas kernels, fill(): pl.pallas_call(fill_kernel, out_shape=jax.ShapeDtypeStruct((NS * NG, 128)...  2.2 us
    pallas_call x1, Pallas kernels, hole_sky(): pl.pallas_call(hole_kernel, out_shape=[jax.ShapeDtypeStruct((NS, HMAX), B...  1.17 us
  transfers between devices with their start and end apart: 7, of which 2 were waited for; matrix products, arithmetic and copies ran while one was open for 0% of the time, Pallas kernels for 13%

profile of v6, /device:TPU:1, one launch (start us, length us, event | category | flops | bytes accessed | tf_op | source)
XLA Modules:
  0.0 39.8 jit_solution(16192633037653976280)
XLA Ops:
  0.0 0.0 copy-start
  0.0 0.0 copy-start.2
  0.0 0.0 copy-start.3
  0.0 0.0 copy-start.4
  0.0 0.0 copy-start.5
  0.0 0.0 copy-start.1
  0.0 4.3 %legendre_sums.1 = bf16[64,2,4,2,128]{4,3,2,1,0:T(2,128)(2,1)} custom-call(bf16[4,64,16,2,128]{4,3,2,1,0:T(2,128)(2,1)} %bitcast.29, bf16[4,2048,256]{2,1,0:T(8,128)(2,1)} %coef.1), custom_call_target="tpu_custom_call" | custom-call | flops 536870912 | bytes 6291456 | tf_op jit(solution)/shard_map/legendre_sums/pallas_call | solution.py:97
  4.4 13.0 %all-to-all-start = ((bf16[64,2,4,2,128]{4,3,2,1,0:T(2,128)(2,1)}), bf16[64,2,4,2,128]{4,3,2,1,0:T(2,128)(2,1)S(1)}, u32[]{:S(2)}, u32[]{:S(2)}) async-start(bf16[64,2,4,2,128]{4,3,2,1,0:T(2,128)(2,1)} %legendre_sums.1), calls=%async_computation | async-start | bytes 524288 | tf_op jit(solution)/shard_map/all_to_all | solution.py:330
  17.4 0.0 copy-done
  17.4 1.4 %collective-permute-start.3 = (bf16[512,256]{1,0:T(8,128)(2,1)S(1)}, bf16[512,256]{1,0:T(8,128)(2,1)S(1)}, u32[]{:S(2)}, u32[]{:S(2)}) collective-permute-start(bf16[512,256]{1,0:T(8,128)(2,1)S(1)} %bitcast.21), channel_id=1, source_target_pairs={{0,1},{1,2},{2,3},{3,0},{4,5},{5,6},{6,7},{7,4},{8,9},{9,10},{10,1... | collective-permute-start | bytes 786440 | tf_op jit(solution)/shard_map/ppermute | solution.py:324
  18.8 2.6 %collective-permute-start.4 = (bf16[512,256]{1,0:T(8,128)(2,1)S(1)}, bf16[512,256]{1,0:T(8,128)(2,1)S(1)}, u32[]{:S(2)}, u32[]{:S(2)}) collective-permute-start(bf16[512,256]{1,0:T(8,128)(2,1)S(1)} %bitcast.22), channel_id=1, source_target_pairs={{0,2},{1,3},{2,0},{3,1},{4,6},{5,7},{6,4},{7,5},{8,10},{9,11},{10,... | collective-permute-start | bytes 786440 | tf_op jit(solution)/shard_map/ppermute | solution.py:324
  21.4 1.1 %collective-permute-start.5 = (bf16[512,256]{1,0:T(8,128)(2,1)S(1)}, bf16[512,256]{1,0:T(8,128)(2,1)S(1)}, u32[]{:S(2)}, u32[]{:S(2)}) collective-permute-start(bf16[512,256]{1,0:T(8,128)(2,1)S(1)} %bitcast.23), channel_id=1, source_target_pairs={{0,3},{1,0},{2,1},{3,2},{4,7},{5,4},{6,5},{7,6},{8,11},{9,8},{10,9... | collective-permute-start | bytes 786440 | tf_op jit(solution)/shard_map/ppermute | solution.py:324
  22.4 0.0 copy-done.2
  22.5 0.0 copy-done.3
  22.5 0.0 copy-done.4
  22.5 0.0 copy-done.5
  22.5 3.9 %prepare.1 = (bf16[256,1024]{1,0:T(8,128)(2,1)S(1)}, bf16[512,1024]{1,0:T(8,128)(2,1)S(1)}, f32[256,128]{1,0:T(8,128)S(1)}, bf16[32,512]{1,0:T(8,128)(2,1)S(1)},...) custom-call(s32[1]{0:T(128)} %bitcast.reg, s32[32,2,128]{2,1,0:T(2,128)S(1)} %bitcast.25, ...), custom_call_target="tpu_custom_call" | custom-call | flops 20000000 | bytes 8388608 | tf_op jit(solution)/shard_map/prepare/pallas_call | solution.py:210
  26.3 4.2 %all-to-all-done = bf16[64,2,4,2,128]{4,3,2,1,0:T(2,128)(2,1)S(1)} async-done(((bf16[64,2,4,2,128]{4,3,2,1,0:T(2,128)(2,1)}), bf16[64,2,4,2,128]{4,3,2,1,0:T(2,128)(2,1)S(1)}, u32[]{:S(2)}, u32[]{:S(2)}) %all-to-all-start) | async-done | bytes 262176 | tf_op jit(solution)/shard_map/all_to_all | solution.py:330
  30.5 0.3 residuals.1
  30.8 1.4 %collective-permute-start = (bf16[64,128]{1,0:T(8,128)(2,1)S(1)}, bf16[64,128]{1,0:T(8,128)(2,1)S(1)}, u32[]{:S(2)}, u32[]{:S(2)}) collective-permute-start(bf16[64,128]{1,0:T(8,128)(2,1)S(1)} %get-tuple-element.20), channel_id=1, source_target_pairs={{0,1},{1,2},{2,3},{3,0},{4,5},{5,6},{6,7},{7,4},{8,9},{9,10},{10,1... | collective-permute-start | bytes 49160 | tf_op jit(solution)/shard_map/ppermute | solution.py:324
  32.2 2.6 %collective-permute-start.1 = (bf16[64,128]{1,0:T(8,128)(2,1)S(1)}, bf16[64,128]{1,0:T(8,128)(2,1)S(1)}, u32[]{:S(2)}, u32[]{:S(2)}) collective-permute-start(bf16[64,128]{1,0:T(8,128)(2,1)S(1)} %get-tuple-element.21), channel_id=1, source_target_pairs={{0,2},{1,3},{2,0},{3,1},{4,6},{5,7},{6,4},{7,5},{8,10},{9,11},{10,... | collective-permute-start | bytes 49160 | tf_op jit(solution)/shard_map/ppermute | solution.py:324
  34.8 0.0 collective-permute-done.3.tile1
  34.8 1.1 %collective-permute-start.2 = (bf16[64,128]{1,0:T(8,128)(2,1)S(1)}, bf16[64,128]{1,0:T(8,128)(2,1)S(1)}, u32[]{:S(2)}, u32[]{:S(2)}) collective-permute-start(bf16[64,128]{1,0:T(8,128)(2,1)S(1)} %get-tuple-element.22), channel_id=1, source_target_pairs={{0,3},{1,0},{2,1},{3,2},{4,7},{5,4},{6,5},{7,6},{8,11},{9,8},{10,9... | collective-permute-start | bytes 49160 | tf_op jit(solution)/shard_map/ppermute | solution.py:324
  35.9 0.0 collective-permute-done.4.tile2
  35.9 0.0 collective-permute-done.5.tile3
  35.9 0.0 copy-done.1
  35.9 1.2 %hole_sky.1 = (bf16[128,512]{1,0:T(8,128)(2,1)S(1)}, bf16[256,512]{1,0:T(8,128)(2,1)S(1)}) custom-call(s32[1]{0:T(128)} %bitcast.reg, s32[1,4]{1,0:T(1,128)S(1)} %copy-done.1, bf16[1024,128]{1,0:T(8,128)(2,1)S(1)} %bitcast.20, bf16[512,1024]{1,0:T(8,128)(2,1)S(1)} %get-tuple-element.23.ph, bf16[512,256]{1,0:T(8,128)(2,1)S(1)} %bitcast.24, ...), custom_call_target="tpu_custom_call" | custom-call | flops 134217728 | bytes 2097152 | tf_op jit(solution)/shard_map/hole_sky/pallas_call | solution.py:260
  37.1 0.0 collective-permute-done.from1
  37.1 0.0 collective-permute-done.1.from2
  37.1 0.5 %collective-permute-done.2.from3 = bf16[64,128]{1,0:T(8,128)(2,1)S(1)} collective-permute-done((bf16[64,128]{1,0:T(8,128)(2,1)S(1)}, bf16[64,128]{1,0:T(8,128)(2,1)S(1)}, u32[]{:S(2)}, u32[]{:S(2)}) %collective-permute-start.2) | collective-permute-done | bytes 16416 | tf_op jit(solution)/shard_map/ppermute | solution.py:324
  37.6 2.2 %fill.1 = bf16[8192,128]{1,0:T(8,128)(2,1)} custom-call(s32[1]{0:T(128)} %bitcast.reg, bf16[64,128]{1,0:T(8,128)(2,1)S(1)} %get-tuple-element.19.after.own, bf16[64,128]{1,0:T(8,128)(2,1)S(1)} %collective-permute-done.from1, bf16[64,128]{1,0:T(8,128)(2,1)S(1)} %collective-permute-done.1.from2, bf16[64,128]{1,0:T(8,128)(2,1)S(1)} %collective-permute-done.2.from3, ...), custom_call_target="tpu_custom_call" | custom-call | flops 1073741824 | bytes 3145728 | tf_op jit(solution)/shard_map/fill/pallas_call | solution.py:302
Async XLA Ops:
  0.0 17.4 %copy-start = (bf16[1,1,512,256]{3,2,1,0:T(8,128)(2,1)S(1)}, bf16[1,1,512,256]{3,2,1,0:T(8,128)(2,1)}, u32[]{:S(2)}) copy-start(bf16[1,1,512,256]{3,2,1,0:T(8,128)(2,1)} %param.15) | copy-start | bytes 786436
  0.0 22.4 %copy-start.2 = (s32[2,4096]{1,0:T(2,128)S(1)}, s32[2,4096]{1,0:T(2,128)}, u32[]{:S(2)}) copy-start(s32[2,4096]{1,0:T(2,128)} %param.12) | copy-start | bytes 98308
  0.0 22.4 %copy-start.3 = (f32[2,4096]{1,0:T(2,128)S(1)}, f32[2,4096]{1,0:T(2,128)}, u32[]{:S(2)}) copy-start(f32[2,4096]{1,0:T(2,128)} %param.11) | copy-start | bytes 98308
  0.0 22.4 %copy-start.4 = (s32[1,4,256]{2,1,0:T(4,128)S(1)}, s32[1,4,256]{2,1,0:T(4,128)}, u32[]{:S(2)}) copy-start(s32[1,4,256]{2,1,0:T(4,128)} %param.13) | copy-start | bytes 12292
  0.0 22.4 %copy-start.5 = (s32[256]{0:T(256)S(1)}, s32[256]{0:T(256)}, u32[]{:S(2)}) copy-start(s32[256]{0:T(256)} %param.10) | copy-start | bytes 3076
  0.0 35.9 %copy-start.1 = (s32[1,4]{1,0:T(1,128)S(1)}, s32[1,4]{1,0:T(1,128)}, u32[]{:S(2)}) copy-start(s32[1,4]{1,0:T(1,128)} %owners.1) | copy-start | bytes 52
  4.4 26.2 %all-to-all-start = ((bf16[64,2,4,2,128]{4,3,2,1,0:T(2,128)(2,1)}), bf16[64,2,4,2,128]{4,3,2,1,0:T(2,128)(2,1)S(1)}, u32[]{:S(2)}, u32[]{:S(2)}) async-start(bf16[64,2,4,2,128]{4,3,2,1,0:T(2,128)(2,1)} %legendre_sums.1), calls=%async_computation | async-start | bytes 524288 | tf_op jit(solution)/shard_map/all_to_all | solution.py:330
  17.4 17.4 %collective-permute-start.3 = (bf16[512,256]{1,0:T(8,128)(2,1)S(1)}, bf16[512,256]{1,0:T(8,128)(2,1)S(1)}, u32[]{:S(2)}, u32[]{:S(2)}) collective-permute-start(bf16[512,256]{1,0:T(8,128)(2,1)S(1)} %bitcast.21), channel_id=1, source_target_pairs={{0,1},{1,2},{2,3},{3,0},{4,5},{5,6},{6,7},{7,4},{8,9},{9,10},{10,1... | collective-permute-start | bytes 786440 | tf_op jit(solution)/shard_map/ppermute | solution.py:324
  18.8 17.1 %collective-permute-start.4 = (bf16[512,256]{1,0:T(8,128)(2,1)S(1)}, bf16[512,256]{1,0:T(8,128)(2,1)S(1)}, u32[]{:S(2)}, u32[]{:S(2)}) collective-permute-start(bf16[512,256]{1,0:T(8,128)(2,1)S(1)} %bitcast.22), channel_id=1, source_target_pairs={{0,2},{1,3},{2,0},{3,1},{4,6},{5,7},{6,4},{7,5},{8,10},{9,11},{10,... | collective-permute-start | bytes 786440 | tf_op jit(solution)/shard_map/ppermute | solution.py:324
  21.4 14.5 %collective-permute-start.5 = (bf16[512,256]{1,0:T(8,128)(2,1)S(1)}, bf16[512,256]{1,0:T(8,128)(2,1)S(1)}, u32[]{:S(2)}, u32[]{:S(2)}) collective-permute-start(bf16[512,256]{1,0:T(8,128)(2,1)S(1)} %bitcast.23), channel_id=1, source_target_pairs={{0,3},{1,0},{2,1},{3,2},{4,7},{5,4},{6,5},{7,6},{8,11},{9,8},{10,9... | collective-permute-start | bytes 786440 | tf_op jit(solution)/shard_map/ppermute | solution.py:324
  30.8 6.3 %collective-permute-start = (bf16[64,128]{1,0:T(8,128)(2,1)S(1)}, bf16[64,128]{1,0:T(8,128)(2,1)S(1)}, u32[]{:S(2)}, u32[]{:S(2)}) collective-permute-start(bf16[64,128]{1,0:T(8,128)(2,1)S(1)} %get-tuple-element.20), channel_id=1, source_target_pairs={{0,1},{1,2},{2,3},{3,0},{4,5},{5,6},{6,7},{7,4},{8,9},{9,10},{10,1... | collective-permute-start | bytes 49160 | tf_op jit(solution)/shard_map/ppermute | solution.py:324
  32.2 4.9 %collective-permute-start.1 = (bf16[64,128]{1,0:T(8,128)(2,1)S(1)}, bf16[64,128]{1,0:T(8,128)(2,1)S(1)}, u32[]{:S(2)}, u32[]{:S(2)}) collective-permute-start(bf16[64,128]{1,0:T(8,128)(2,1)S(1)} %get-tuple-element.21), channel_id=1, source_target_pairs={{0,2},{1,3},{2,0},{3,1},{4,6},{5,7},{6,4},{7,5},{8,10},{9,11},{10,... | collective-permute-start | bytes 49160 | tf_op jit(solution)/shard_map/ppermute | solution.py:324
  34.8 2.8 %collective-permute-start.2 = (bf16[64,128]{1,0:T(8,128)(2,1)S(1)}, bf16[64,128]{1,0:T(8,128)(2,1)S(1)}, u32[]{:S(2)}, u32[]{:S(2)}) collective-permute-start(bf16[64,128]{1,0:T(8,128)(2,1)S(1)} %get-tuple-element.22), channel_id=1, source_target_pairs={{0,3},{1,0},{2,1},{3,2},{4,7},{5,4},{6,5},{7,6},{8,11},{9,8},{10,9... | collective-permute-start | bytes 49160 | tf_op jit(solution)/shard_map/ppermute | solution.py:324
